TPU v7x, 32 devices: a whole 2x2x4 slice. The times are simulated.
32 devices in a mesh: tm: 8 (over z, y), dp: 4 (over x, core).
Axes of the slice: x: 2, y: 2, z: 4, core: 2. Of those that a mesh axis runs over, the one named last changes fastest.
Arguments:
- inputs: bfloat16 [4, 8192, 1024], P('dp', 'tm'), may hold values from -6 to 6
- weights: bfloat16 [1024, 1536], replicated, may hold values from -0.1875 to 0.1875
- out_grad: bfloat16 [4, 8192, 512], P('dp', 'tm'), may hold values from -6 to 6
Outputs:
- input_grad: bfloat16 [4, 8192, 1024], P('dp', 'tm')
- weight_grad: float32 [1024, 1536], P('tm')
All inputs are finite; a program needn't handle non-finite values.
Results may differ from a plain program's by a relative error of at most 0.0075.
Values sent between devices are 32-bit elements; how exact they have to be, the bound alone decides.
A program may use at most 128 MiB of HBM per device.

v0:
```python
import jax
import jax.numpy as jnp
from jax import lax
from jax.sharding import PartitionSpec as P

H = 4
HD = 128
CH = 256


def carried_in(value, axis, join, neutral, backward):
    count, mine = (lax.axis_size(axis), lax.axis_index(axis))
    pieces = lax.all_gather(value, axis)
    if backward:
        pieces = pieces[::-1]
        mine = count - 1 - mine
    so_far = jnp.full_like(value, 0) + jnp.asarray(neutral, value.dtype)

    def lap(position, so_far):
        longer = join(so_far, pieces[position])
        return jnp.where(position < mine, longer, so_far)

    return lax.fori_loop(0, count - 1, lap, so_far)


def combine(earlier, later):
    return jax.tree.map(jnp.add, earlier, later)


def shards(inputs, weights, out_grad):
    f32 = jnp.float32
    bf16 = jnp.bfloat16
    tok_count = inputs.shape[1]
    width = weights.shape[1] // 3
    block_count = tok_count // CH
    record = inputs[0]
    qkv = jnp.dot(record, weights, preferred_element_type=f32).astype(bf16)
    shape4 = (block_count, CH, H, HD)
    queries = qkv[:, :width].reshape(shape4)
    key_rows = qkv[:, width : 2 * width].reshape(shape4)
    values = qkv[:, 2 * width :].reshape(shape4)
    offset = lax.axis_index("tm") * tok_count
    position = (offset + jnp.arange(tok_count, dtype=jnp.int32)).astype(f32)
    factor = 1.0 / jnp.sqrt(jnp.float32(HD) * (position + 1.0))
    scaled_grad = (out_grad[0].astype(f32) * factor[:, None]).astype(bf16).reshape(shape4)
    tri = (
        lax.broadcasted_iota(jnp.int32, (CH, CH), 0) >= lax.broadcasted_iota(jnp.int32, (CH, CH), 1)
    ).astype(f32)
    kv_group = jnp.einsum("nshd,nshe->nhde", key_rows, values, preferred_element_type=f32)
    qg_group = jnp.einsum("nthd,nthe->nhde", queries, scaled_grad, preferred_element_type=f32)
    kv_device = jnp.sum(kv_group, 0)
    qg_device = jnp.sum(qg_group, 0)
    zeros = jnp.zeros((H, HD, HD), f32)
    state_start = carried_in(kv_device, "tm", combine, zeros, False)
    grad_end = carried_in(qg_device, "tm", combine, zeros, True)
    mix_vg = (
        jnp.einsum("nthe,nshe->nhts", scaled_grad, values, preferred_element_type=f32) * tri
    ).astype(bf16)
    mix_qk = (
        jnp.einsum("nthd,nshd->nhts", queries, key_rows, preferred_element_type=f32) * tri
    ).astype(bf16)
    state_before = (state_start[None] + jnp.cumsum(kv_group, 0) - kv_group).astype(bf16)
    grad_after = (
        grad_end[None] + jnp.flip(jnp.cumsum(jnp.flip(qg_group, 0), 0), 0) - qg_group
    ).astype(bf16)
    grad_q = jnp.einsum(
        "nhts,nshd->nthd", mix_vg, key_rows, preferred_element_type=f32
    ) + jnp.einsum("nthe,nhde->nthd", scaled_grad, state_before, preferred_element_type=f32)
    grad_k = jnp.einsum(
        "nhts,nthd->nshd", mix_vg, queries, preferred_element_type=f32
    ) + jnp.einsum("nshe,nhde->nshd", values, grad_after, preferred_element_type=f32)
    grad_v = jnp.einsum(
        "nhts,nthe->nshe", mix_qk, scaled_grad, preferred_element_type=f32
    ) + jnp.einsum("nshd,nhde->nshe", key_rows, grad_after, preferred_element_type=f32)
    dqkv = jnp.concatenate(
        [
            grad_q.reshape(tok_count, width),
            grad_k.reshape(tok_count, width),
            grad_v.reshape(tok_count, width),
        ],
        axis=1,
    ).astype(bf16)
    record_grad = lax.dot_general(
        dqkv, weights, (((1,), (1,)), ((), ())), preferred_element_type=f32
    ).astype(bf16)
    partial_rows = lax.psum_scatter(
        lax.dot_general(record, dqkv, (((0,), (0,)), ((), ())), preferred_element_type=f32),
        "tm",
        scatter_dimension=0,
        tiled=True,
    )
    proj_grad = lax.psum(partial_rows, "dp")
    return (record_grad[None], proj_grad)


def solution(mesh):
    placed = (P("dp", "tm", None), P(), P("dp", "tm", None))
    return jax.shard_map(
        shards,
        mesh=mesh,
        in_specs=placed,
        out_specs=(P("dp", "tm", None), P("tm", None)),
        check_vma=False,
    )
```

profile of v0, /device:TPU:0, one launch (start us, length us, event | category | flops | bytes accessed | tf_op | source)
XLA Modules:
  0.0 325.1 jit_solution(12180927547092387833)
XLA Ops:
  7.2 2.8 reshape.58
  10.1 2.9 copy.36
  13.0 5.2 %convolution_convert_fusion = bf16[1024,1536]{1,0:T(8,128)(2,1)S(1)} fusion(bf16[1024,1536]{1,0:T(8,128)(2,1)S(1)} %copy-done, bf16[1,1024,1024]{2,1,0:T(8,128)(2,1)} %param.7), kind=kOutput, calls=%fused_computation.5 | convolution fusion | flops 3222798336 | bytes 8388608 | tf_op jit(solution)/shard_map/dot_general | solution.py:37
  18.2 1.7 fusion.25
  19.9 2.2 reshape.55
  22.2 1.9 multiply_convert_fusion.2
  25.1 2.2 fusion.27
  27.3 2.2 reshape.53
  29.5 2.2 reshape.52
  31.7 3.8 %fusion.26 = (f32[4,128,128]{2,1,0:T(8,128)}, f32[4,4,128,128]{3,2,1,0:T(8,128)}) fusion(bf16[4,256,4,128]{3,2,1,0:T(4,128)(2,1)} %reshape.53, bf16[4,256,4,128]{3,2,1,0:T(4,128)(2,1)} %reshape.52), kind=kOutput, calls=%fused_computation.42 | convolution fusion | flops 134414336 | bytes 3407872 | tf_op jit(solution)/shard_map/nshd,nshe->nhde/dot_general | solution.py:49
  36.5 2.3 rev.11
  38.8 2.4 fusion.28
  41.3 1.8 multiply_convert_fusion.1
  43.1 1.9 fusion.10
  45.0 2.2 fusion.19
  47.1 4.2 %fusion.2 = f32[4,4,128,256]{3,2,1,0:T(8,128)} fusion(bf16[4,256,4,128]{1,3,2,0:T(8,128)(2,1)} %copy-done.1, f32[256,256]{1,0:T(8,128)} %fusion.24, bf16[4,256,4,128]{3,2,1,0:T(4,128)(2,1)} %reshape.55, bf16[4,256,4,128]{3,2,1,0:T(4,128)(2,1)} %reshape.52), kind=kOutput, calls=%fused_computation.13 | convolution fusion | flops 538968064 | bytes 5505024 | tf_op jit(solution)/shard_map/nhts,nthe->nshe/dot_general | solution.py:72
  51.4 28.0 %all-gather.7.cloned.1.call-done = f32[32,128,128]{2,1,0:T(8,128)} async-done(((f32[4,128,128]{2,1,0:T(8,128)}), f32[32,128,128]{2,1,0:T(8,128)}) %all-gather.7.cloned.1.call-update) | async-done | bytes 2097168 | tf_op jit(solution)/shard_map/all_gather | solution.py:13
  79.4 3.2 rev.10
  82.6 12.3 %while.29 = (s32[]{:T(128)}, f32[4,128,128]{2,1,0:T(8,128)}, s32[]{:T(128)}, f32[8,4,128,128]{3,2,1,0:T(8,128)}, s32[]{:T(128)}, /*index=5*/s32[]{:T(128)}) while((s32[]{:T(128)}, f32[4,128,128]{2,1,0:T(8,128)}, s32[]{:T(128)}, f32[8,4,128,128]{3,2,1,0:T(8,128)}, s32[]{:T(128)}, /*index=5*/s32[]{:T(128)}) %tuple.73), condition=%wide.region_6.7_spmd.clone, body=%wide.region_5.6_spmd.clone.sunk | while | flops 196612 | bytes 786525 | solution.py:23
  82.6 1.7 add_select_fusion.5
  84.3 1.8 add_select_fusion.5
  86.0 1.8 add_select_fusion.5
  87.8 1.8 add_select_fusion.5
  89.6 1.8 add_select_fusion.5
  91.4 1.8 add_select_fusion.5
  93.1 1.8 add_select_fusion.5
  94.9 1.8 subtract_convert_fusion
  97.5 3.1 fusion.5
  100.6 2.4 copy.48
  102.9 26.4 %all-gather.5.cloned.1.call-done = f32[32,128,128]{2,1,0:T(8,128)} async-done(((f32[4,128,128]{2,1,0:T(8,128)}), f32[32,128,128]{2,1,0:T(8,128)}) %all-gather.5.cloned.1.call-update) | async-done | bytes 2097168 | tf_op jit(solution)/shard_map/all_gather | solution.py:13
  129.4 7.4 %while.28 = (s32[]{:T(128)}, f32[4,128,128]{2,1,0:T(8,128)S(1)}, s32[]{:T(128)}, f32[8,4,128,128]{3,2,1,0:T(8,128)}, s32[]{:T(128)}, /*index=5*/s32[]{:T(128)}) while((s32[]{:T(128)}, f32[4,128,128]{2,1,0:T(8,128)S(1)}, s32[]{:T(128)}, f32[8,4,128,128]{3,2,1,0:T(8,128)}, s32[]{:T(128)}, /*index=5*/s32[]{:T(128)}) %tuple.84), condition=%wide.region_2.3_spmd.clone, body=%wide.region_1.0_spmd.clone.sunk | while | flops 196612 | bytes 786525 | solution.py:23
  130.4 1.0 add_select_fusion.4
  131.5 1.0 add_select_fusion.4
  132.5 1.0 add_select_fusion.4
  134.7 1.0 add_select_fusion.4
  136.8 1.8 fusion.7
  138.6 3.0 fusion.4
  141.7 2.3 copy.43
  144.0 2.6 bitcast_dynamic-update-slice_fusion.2
  146.6 3.1 fusion.6
  149.7 2.3 copy.53
  152.0 2.6 bitcast_dynamic-update-slice_fusion.1
  154.6 1.3 bitcast_dynamic-update-slice_fusion
  155.8 7.4 %convolution_bitcast_fusion = f32[1024,1536]{0,1:T(8,128)} fusion(bf16[1024,1536]{1,0:T(8,128)(2,1)} %bitcast_dynamic-update-slice_fusion, bf16[1,1024,1024]{2,1,0:T(8,128)(2,1)S(1)} %copy-done.13), kind=kOutput, calls=%fused_computation.2 | convolution fusion | flops 3221225472 | bytes 11534336 | tf_op jit(solution)/shard_map/dot_general | solution.py:87
  163.3 117.0 %reduce-scatter.2.cloned.1.call-done = f32[128,1536]{0,1:T(8,128)} async-done(((f32[1024,1536]{0,1:T(8,128)}), f32[128,1536]{0,1:T(8,128)}) %reduce-scatter.2.cloned.1.call-update) | async-done | bytes 786448 | tf_op jit(solution)/shard_map/reduce_scatter | solution.py:86
  280.3 6.5 %convert_bitcast_fusion = bf16[1,1024,1024]{2,1,0:T(8,128)(2,1)} fusion(bf16[1024,1536]{1,0:T(8,128)(2,1)} %bitcast_dynamic-update-slice_fusion, bf16[1024,1536]{1,0:T(8,128)(2,1)S(1)} %copy-done), kind=kOutput, calls=%fused_computation.8 | convolution fusion | flops 3222274048 | bytes 8388608 | tf_op jit(solution)/shard_map/dot_general | solution.py:83
  286.8 29.5 %all-reduce.2.cloned.1.call-done = f32[128,1536]{0,1:T(8,128)} async-done(((f32[128,1536]{0,1:T(8,128)}), f32[128,1536]{0,1:T(8,128)}) %all-reduce.2.cloned.1.call-update) | async-done | bytes 786448 | tf_op jit(solution)/shard_map/psum | solution.py:92
  316.3 2.3 copy.54
  (43 shorter events, 6.1 us)
Async XLA Ops:
  7.2 5.8 %copy-start = (bf16[1024,1536]{1,0:T(8,128)(2,1)S(1)}, bf16[1024,1536]{1,0:T(8,128)(2,1)}, u32[]{:S(2)}) copy-start(bf16[1024,1536]{1,0:T(8,128)(2,1)} %param.8) | copy-start | bytes 9437188
  7.2 72.2 %all-gather.7.cloned.1.call-start = ((), (), s32[]{:S(2)}) async-start(), calls=%async_computation.4 | async-start | bytes 2359296 | tf_op jit(solution)/shard_map/all_gather | solution.py:13
  22.2 2.9 copy-start.8
  24.1 1.0 copy-start.1
  27.3 102.1 %all-gather.5.cloned.1.call-start = ((), (), s32[]{:S(2)}) async-start(), calls=%async_computation.3 | async-start | bytes 2359296 | tf_op jit(solution)/shard_map/all_gather | solution.py:13
  35.5 244.7 %reduce-scatter.2.cloned.1.call-start = ((), (), s32[]{:S(2)}) async-start(), calls=%async_computation.1 | async-start | bytes 7077888 | tf_op jit(solution)/shard_map/reduce_scatter | solution.py:86
  38.8 2.4 copy-start.2
  38.8 2.4 copy-start.6
  41.3 1.8 copy-start.9
  43.1 1.9 copy-start.4
  94.9 2.6 copy-start.7
  96.7 0.8 copy-start.10
  136.8 1.9 copy-start.3
  144.0 2.6 copy-start.5
  144.0 2.6 copy-start.11
  152.0 2.6 copy-start.12
  152.0 3.8 %copy-start.13 = (bf16[1,1024,1024]{2,1,0:T(8,128)(2,1)S(1)}, bf16[1,1024,1024]{2,1,0:T(8,128)(2,1)}, u32[]{:S(2)}) copy-start(bf16[1,1024,1024]{2,1,0:T(8,128)(2,1)} %param.7) | copy-start | bytes 6291460
  163.2 153.0 %all-reduce.2.cloned.1.call-start = ((), (), s32[]{:S(2)}) async-start(), calls=%async_computation.2 | async-start | bytes 1572864 | tf_op jit(solution)/shard_map/psum | solution.py:92
Sparse Core Ops, SparseCore 0:
  27.4 51.9 all-gather.6
  81.5 47.7 all-gather.4
  163.3 116.8 reduce-scatter.1
  282.5 33.7 all-reduce.1
where the time goes:
time: 326 us; the launch traced here: 325 us
  waiting for transfers between devices  201 us (62%)
  matrix products  44.4 us (14%)
  local copies, waits for them, and re-layouts  37.1 us (11%)
  other arithmetic  28.2 us (9%)
  between operations  13.9 us (4%)
    reduce_scatter x1, waiting for transfers between devices, shards(): lax.psum_scatter(lax.dot_general(record, dqkv, (((0,), (0,)), ((), ())),...  117 us
    all_gather x2, waiting for transfers between devices, carried_in(): pieces = lax.all_gather(value, axis)  54.5 us
    psum x1, waiting for transfers between devices, shards(): proj_grad = lax.psum(partial_rows, 'dp')  29.5 us
    select_n x14, other arithmetic, lap(): return jnp.where(position < mine, longer, so_far)  19.6 us
    unnamed x31, local copies, waits for them, and re-layouts  9.28 us
    dot_general x1, matrix products, shards(): lax.dot_general(record, dqkv, (((0,), (0,)), ((), ())), preferred_element...  7.36 us
    dot_general x1, matrix products, shards(): lax.dot_general(dqkv, weights, (((1,), (1,)), ((), ())), preferred_elemen...  6.53 us
  transfers between devices with their start and end apart: 4, of which 4 were waited for; matrix products, arithmetic and copies ran while one was open for 16% of the time, Pallas kernels for 0%

commit v1 on v0

v1 whole, which is shorter than its diff:
```python
import functools

import jax
import jax.numpy as jnp
from jax import lax
from jax.experimental import pallas as pl
from jax.experimental.pallas import tpu as pltpu
from jax.sharding import PartitionSpec as P

H = 4
HD = 128
CH = 256
MESH = pl.DeviceIdType.MESH
F32 = jnp.float32
BF16 = jnp.bfloat16
NN = (((1,), (0,)), ((), ()))
NT = (((1,), (1,)), ((), ()))
TN = (((0,), (0,)), ((), ()))


def mm(a, b, dims=NN):
    return lax.dot_general(a, b, dims, preferred_element_type=F32)


def kernel(
    sizes,
    x_ref, w_ref, og_ref, dx_ref, dw_ref,
    qkv, sc, kvg, qgg, loc, dqkv, xt,
    kst, qst, kyr, qyr,
    part, crecv, a_xr, a_yr, a2, a_zr, ga, b_yr, b_zr, b2, b_xr, b3, gb,
    zk_s, zk_r, zq_s, zq_r, yk_s, yk_r, yq_s, yq_r,
    c_s, c_r, ax_s, ax_r, ay_s, ay_r, az_s, az_r, ag_s, ag_r,
    by_s, by_r, bz_s, bz_r, bx_s, bx_r, gb_s, gb_r,
):
    nz, ny, nx = sizes
    tok = x_ref.shape[0]
    nb = tok // CH
    width = H * HD
    rx = dw_ref.shape[0] // nx
    tm, dp = lax.axis_index("tm"), lax.axis_index("dp")
    z, y = tm // ny, lax.rem(tm, ny)
    x, c = dp // 2, lax.rem(dp, 2)

    def at(z_=None, y_=None, x_=None, c_=None):
        z_ = z if z_ is None else z_
        y_ = y if y_ is None else y_
        x_ = x if x_ is None else x_
        c_ = c if c_ is None else c_
        return (z_ * ny + y_, x_ * 2 + c_)

    def zpeer(d):
        return lax.rem(z + d, nz)

    def ypeer(d):
        return lax.rem(y + d, ny)

    def xpeer(d):
        return lax.rem(x + d, nx)

    def remote(src, dst, send, recv, device):
        return pltpu.make_async_remote_copy(
            src_ref=src, dst_ref=dst, send_sem=send, recv_sem=recv,
            device_id=device, device_id_type=MESH,
        )

    def head(p):
        return lax.rem(p + (H // 2) * (1 - c), H)

    peers = [at(c_=1 - c)]
    for d in range(1, nx):
        peers += [at(x_=xpeer(d)), at(x_=xpeer(d), c_=1 - c)]
    peers += [at(y_=ypeer(d)) for d in range(1, ny)]
    peers += [at(z_=zpeer(d)) for d in range(1, nz)]
    barrier = pltpu.get_barrier_semaphore()
    for peer in peers:
        pl.semaphore_signal(barrier, inc=1, device_id=peer, device_id_type=MESH)

    def project(n, carry):
        rows = pl.ds(pl.multiple_of(n * CH, CH), CH)
        r = mm(x_ref[rows, :], w_ref[...]).astype(BF16)
        pos = tm * tok + n * CH + lax.broadcasted_iota(jnp.int32, (CH, 1), 0)
        factor = 1.0 / jnp.sqrt(jnp.float32(HD) * (pos.astype(F32) + 1.0))
        g = (og_ref[rows, :].astype(F32) * factor).astype(BF16)
        for h in range(H):
            q = r[:, h * HD : (h + 1) * HD]
            k = r[:, width + h * HD : width + (h + 1) * HD]
            v = r[:, 2 * width + h * HD : 2 * width + (h + 1) * HD]
            s = g[:, h * HD : (h + 1) * HD]
            qkv[0, h, rows, :] = q
            qkv[1, h, rows, :] = k
            qkv[2, h, rows, :] = v
            sc[h, rows, :] = s
            kvg[n, h] = mm(k, v, TN)
            qgg[n, h] = mm(q, s, TN)
        return carry

    lax.fori_loop(0, nb, project, 0)

    pl.semaphore_wait(barrier, len(peers))

    @pl.when(z == 0)
    def _():
        kst[0] = jnp.zeros_like(kst[0])

    @pl.when(z == nz - 1)
    def _():
        qst[0] = jnp.zeros_like(qst[0])

    def link(p, ord_, last, nxt, st, grp, zs, zr, ys, yr_, ybuf, later):
        @pl.when(ord_ > 0)
        def _():
            remote(st.at[1, p], st.at[0, p], zs.at[p], zr.at[p], at(z_=z)).wait_recv()

        hh = head(p)
        total = st[0, p]
        for n in range(nb):
            total = total + grp[n, hh]
        st[1, p] = total

        @pl.when(ord_ < nz - 1)
        def _():
            remote(st.at[1, p], st.at[0, p], zs.at[p], zr.at[p], at(z_=nxt)).start()

        for d in range(1, ny):
            other = ypeer(d)
            which = jnp.where(later(other), 1, 0)
            remote(
                st.at[which, p], ybuf.at[d - 1, p], ys.at[d - 1, p], yr_.at[d - 1, p],
                at(y_=other),
            ).start()

    def local(n, p):
        hh = head(p)
        rows = pl.ds(pl.multiple_of(n * CH, CH), CH)
        q, k, v, s = qkv[0, hh, rows, :], qkv[1, hh, rows, :], qkv[2, hh, rows, :], sc[hh, rows, :]
        row = lax.broadcasted_iota(jnp.int32, (CH, CH), 0)
        col = lax.broadcasted_iota(jnp.int32, (CH, CH), 1)
        low, up = row >= col, row <= col
        vg = jnp.where(low, mm(s, v, NT), 0.0).astype(BF16)
        vgt = jnp.where(up, mm(v, s, NT), 0.0).astype(BF16)
        qkt = jnp.where(up, mm(k, q, NT), 0.0).astype(BF16)
        loc[0, p, rows, :] = mm(vg, k)
        loc[1, p, rows, :] = mm(vgt, q)
        loc[2, p, rows, :] = mm(qkt, s)

    steps = nz + H - 1
    items = nb * H + nb
    per = -(-items // steps)

    def step(i, carry):
        kp = i - z
        qp = i - (nz - 1 - z)

        @pl.when((kp >= 0) & (kp < H))
        def _():
            link(kp, z, nz, z + 1, kst, kvg, zk_s, zk_r, yk_s, yk_r, kyr, lambda o: o > y)

        @pl.when((qp >= 0) & (qp < H))
        def _():
            link(qp, nz - 1 - z, nz, z - 1, qst, qgg, zq_s, zq_r, yq_s, yq_r, qyr, lambda o: o < y)

        def piece(u, carry):
            idx = i * per + u

            @pl.when(idx < nb * H)
            def _():
                local(lax.rem(idx, nb), idx // nb)

            @pl.when((idx >= nb * H) & (idx < items))
            def _():
                rows = pl.ds(pl.multiple_of((idx - nb * H) * CH, CH), CH)
                xt[:, rows] = x_ref[rows, :].T

            return carry

        return lax.fori_loop(0, per, piece, carry)

    lax.fori_loop(0, steps, step, 0)

    zero = jnp.int32(0)

    def core_copy(stream, j):
        return remote(part.at[stream, j], crecv.at[stream, j], c_s.at[stream, j], c_r.at[stream, j], at(c_=1 - c))

    def ax_copy(d, j):
        o = xpeer(d)
        return remote(part.at[2, j, :, :, o], a_xr.at[d - 1, j], ax_s.at[d - 1, j], ax_r.at[d - 1, j], at(x_=o))

    def by_copy(d, j):
        o = ypeer(d)
        return remote(part.at[3, j, :, o], b_yr.at[d - 1, j], by_s.at[d - 1, j], by_r.at[d - 1, j], at(y_=o))

    def ay_copy(d, j):
        o = ypeer(d)
        return remote(part.at[2, j, :, o, x], a_yr.at[d - 1, j], ay_s.at[d - 1, j], ay_r.at[d - 1, j], at(y_=o))

    def az_copy(d, j):
        o = zpeer(d)
        return remote(a2.at[j, o], a_zr.at[d - 1, j], az_s.at[d - 1, j], az_r.at[d - 1, j], at(z_=o))

    def bz_copy(d, j):
        o = zpeer(d)
        return remote(part.at[3, j, o, y], b_zr.at[d - 1, j], bz_s.at[d - 1, j], bz_r.at[d - 1, j], at(z_=o))

    def bx_copy(d, j):
        o = xpeer(d)
        return remote(b2.at[j], b_xr.at[d - 1, j], bx_s.at[d - 1, j], bx_r.at[d - 1, j], at(x_=o))

    def gb_copy(j):
        return remote(b3.at[j], gb.at[j], gb_s.at[j], gb_r.at[j], at(c_=1 - c))

    def ag_copy(e, j):
        d, flip = e // 2, e % 2
        o = xpeer(d)
        oc = 1 - c if flip else c
        return remote(ga.at[0, j], ga.at[e, j], ag_s.at[e, j], ag_r.at[e, j], at(x_=o, c_=oc))

    def finish(p):
        hh = head(p)
        start, end = kst[0, p], qst[0, p]
        for d in range(1, ny):
            remote(kst.at[0, p], kyr.at[d - 1, p], yk_s.at[d - 1, p], yk_r.at[d - 1, p], at(y_=ypeer(d))).wait_recv()
            remote(qst.at[0, p], qyr.at[d - 1, p], yq_s.at[d - 1, p], yq_r.at[d - 1, p], at(y_=ypeer(d))).wait_recv()
            start = start + kyr[d - 1, p]
            end = end + qyr[d - 1, p]
        cols = [pl.ds(pl.multiple_of(j * width + hh * HD, HD), HD) for j in range(3)]
        for n in range(nb):
            rows = pl.ds(n * CH, CH)
            dq = loc[0, p, rows, :] + mm(sc[hh, rows, :], start.astype(BF16), NT)
            dqkv[rows, cols[0]] = dq.astype(BF16)
            start = start + kvg[n, hh]
        for n in range(nb - 1, -1, -1):
            rows = pl.ds(n * CH, CH)
            after = end.astype(BF16)
            dk = loc[1, p, rows, :] + mm(qkv[2, hh, rows, :], after, NT)
            dv = loc[2, p, rows, :] + mm(qkv[1, hh, rows, :], after)
            dqkv[rows, cols[1]] = dk.astype(BF16)
            dqkv[rows, cols[2]] = dv.astype(BF16)
            end = end + qgg[n, hh]
        d = jnp.concatenate([dqkv[:, cols[j]] for j in range(3)], axis=1)
        dm = xt.shape[0]
        m = 256
        zrows = dm // nz

        def slab(i, carry):
            rows = pl.ds(pl.multiple_of(i * zrows, zrows), zrows)
            r = mm(xt[rows, :], d)
            for j in range(3):
                part[p, j, i] = r[:, j * HD : (j + 1) * HD].reshape(ny, nx, rx, HD)
            return carry

        lax.fori_loop(0, nz, slab, 0)

    def head_step(p, carry):
        finish(p)

        @pl.when(p < 2)
        def _():
            for j in range(3):
                core_copy(p, j).start()

        @pl.when(p >= 2)
        def _():
            for j in range(3):
                core_copy(p - 2, j).wait_recv()
                for i in range(nz):
                    part[p, j, i] = part[p, j, i] + crecv[p - 2, j, i]

                @pl.when(p == 2)
                def _():
                    for d in range(1, nx):
                        ax_copy(d, j).start()

                @pl.when(p == 3)
                def _():
                    for d in range(1, ny):
                        by_copy(d, j).start()

        return carry

    lax.fori_loop(0, H, head_step, 0)

    def input_rows(i, carry):
        rows = pl.ds(pl.multiple_of(i * CH, CH), CH)
        dx_ref[rows, :] = mm(dqkv[rows, :], w_ref[...], NT).astype(BF16)
        return carry

    lax.fori_loop(0, nb, input_rows, 0)

    def stage1(j, carry):
        for d in range(1, nx):
            ax_copy(d, j).wait_recv()
        for i in range(nz):
            t = part[2, j, i, :, x]
            for d in range(1, nx):
                t = t + a_xr[d - 1, j, i]
            part[2, j, i, :, x] = t
        for d in range(1, ny):
            ay_copy(d, j).start()
        for d in range(1, ny):
            by_copy(d, j).wait_recv()
        for i in range(nz):
            t = part[3, j, i, y]
            for d in range(1, ny):
                t = t + b_yr[d - 1, j, i]
            part[3, j, i, y] = t
        for d in range(1, nz):
            bz_copy(d, j).start()
        return carry

    def stage2(j, carry):
        for d in range(1, ny):
            ay_copy(d, j).wait_recv()
        for i in range(nz):
            t = part[2, j, i, y, x]
            for d in range(1, ny):
                t = t + a_yr[d - 1, j, i]
            a2[j, i] = t
        for d in range(1, nz):
            az_copy(d, j).start()
        for d in range(1, nz):
            bz_copy(d, j).wait_recv()
        t = part[3, j, z, y]
        for d in range(1, nz):
            t = t + b_zr[d - 1, j]
        b2[j] = t
        for d in range(1, nx):
            bx_copy(d, j).start()
        return carry

    def stage3(j, carry):
        for d in range(1, nz):
            az_copy(d, j).wait_recv()
        t = a2[j, z]
        for d in range(1, nz):
            t = t + a_zr[d - 1, j]
        ga[0, j] = t
        for e in range(1, 2 * nx):
            ag_copy(e, j).start()
        for d in range(1, nx):
            bx_copy(d, j).wait_recv()
        t = b2[j]
        for d in range(1, nx):
            t = t + b_xr[d - 1, j]
        b3[j] = t
        gb_copy(j).start()
        cols = pl.ds(pl.multiple_of(j * width + (2 * c + 1) * HD, HD), HD)
        dw_ref[:, cols] = t.reshape(nx * rx, HD)
        return carry

    def stage4(j, carry):
        for e in range(2 * nx):
            if e:
                ag_copy(e, j).wait_recv()
            d, flip = e // 2, e % 2
            o = lax.rem(x - d + nx, nx)
            oc = 1 - c if flip else c
            rows = pl.ds(pl.multiple_of(o * rx, rx), rx)
            cols = pl.ds(pl.multiple_of(j * width + 2 * oc * HD, HD), HD)
            dw_ref[rows, cols] = ga[e, j]
        gb_copy(j).wait_recv()
        cols = pl.ds(pl.multiple_of(j * width + (2 * (1 - c) + 1) * HD, HD), HD)
        dw_ref[:, cols] = gb[j].reshape(nx * rx, HD)
        return carry

    lax.fori_loop(0, 3, stage1, 0)
    lax.fori_loop(0, 3, stage2, 0)
    lax.fori_loop(0, 3, stage3, 0)
    lax.fori_loop(0, 3, stage4, 0)

    def drain_state(p, carry):
        @pl.when(z < nz - 1)
        def _():
            remote(kst.at[1, p], kst.at[0, p], zk_s.at[p], zk_r.at[p], at(z_=z)).wait_send()

        @pl.when(z > 0)
        def _():
            remote(qst.at[1, p], qst.at[0, p], zq_s.at[p], zq_r.at[p], at(z_=z)).wait_send()

        for d in range(1, ny):
            remote(kst.at[0, p], kyr.at[d - 1, p], yk_s.at[d - 1, p], yk_r.at[d - 1, p], at(y_=ypeer(d))).wait_send()
            remote(qst.at[0, p], qyr.at[d - 1, p], yq_s.at[d - 1, p], yq_r.at[d - 1, p], at(y_=ypeer(d))).wait_send()
        return carry

    def drain(j, carry):
        core_copy(0, j).wait_send()
        core_copy(1, j).wait_send()
        for d in range(1, nx):
            ax_copy(d, j).wait_send()
            bx_copy(d, j).wait_send()
        for d in range(1, ny):
            ay_copy(d, j).wait_send()
            by_copy(d, j).wait_send()
        for d in range(1, nz):
            az_copy(d, j).wait_send()
            bz_copy(d, j).wait_send()
        for e in range(1, 2 * nx):
            ag_copy(e, j).wait_send()
        gb_copy(j).wait_send()
        return carry

    lax.fori_loop(0, H, drain_state, 0)
    lax.fori_loop(0, 3, drain, 0)


def shards(nz, ny, nx, inputs, weights, out_grad):
    record, cot = inputs[0], out_grad[0]
    tok, dm = record.shape
    nb = tok // CH
    rx = dm // (nz * ny * nx)
    V = pltpu.VMEM
    D = pltpu.SemaphoreType.DMA
    scratch = [
        V((3, H, tok, HD), BF16), V((H, tok, HD), BF16),
        V((nb, H, HD, HD), F32), V((nb, H, HD, HD), F32),
        V((3, H, tok, HD), F32), V((tok, 3 * H * HD), BF16), V((dm, tok), BF16),
        V((2, H, HD, HD), F32), V((2, H, HD, HD), F32),
        V((ny - 1, H, HD, HD), F32), V((ny - 1, H, HD, HD), F32),
        V((4, 3, nz, ny, nx, rx, HD), F32), V((2, 3, nz, ny, nx, rx, HD), F32),
        V((nx - 1, 3, nz, ny, rx, HD), F32), V((ny - 1, 3, nz, rx, HD), F32),
        V((3, nz, rx, HD), F32), V((nz - 1, 3, rx, HD), F32), V((2 * nx, 3, rx, HD), F32),
        V((ny - 1, 3, nz, nx, rx, HD), F32), V((nz - 1, 3, nx, rx, HD), F32),
        V((3, nx, rx, HD), F32), V((nx - 1, 3, nx, rx, HD), F32),
        V((3, nx, rx, HD), F32), V((3, nx, rx, HD), F32),
        D((H,)), D((H,)), D((H,)), D((H,)),
        D((ny - 1, H)), D((ny - 1, H)), D((ny - 1, H)), D((ny - 1, H)),
        D((2, 3)), D((2, 3)), D((nx - 1, 3)), D((nx - 1, 3)), D((ny - 1, 3)), D((ny - 1, 3)),
        D((nz - 1, 3)), D((nz - 1, 3)), D((2 * nx, 3)), D((2 * nx, 3)),
        D((ny - 1, 3)), D((ny - 1, 3)), D((nz - 1, 3)), D((nz - 1, 3)),
        D((nx - 1, 3)), D((nx - 1, 3)), D((3,)), D((3,)),
    ]
    vm = pl.BlockSpec(memory_space=pltpu.VMEM)
    dx, dw = pl.pallas_call(
        functools.partial(kernel, (nz, ny, nx)),
        out_shape=(
            jax.ShapeDtypeStruct((tok, dm), BF16),
            jax.ShapeDtypeStruct((dm // (nz * ny), weights.shape[1]), F32),
        ),
        in_specs=[vm, vm, vm],
        out_specs=(vm, vm),
        scratch_shapes=scratch,
        compiler_params=pltpu.CompilerParams(
            collective_id=0, has_side_effects=True, vmem_limit_bytes=60 * 1024 * 1024
        ),
    )(record, weights, cot)
    return dx[None], dw


def solution(mesh):
    nx = mesh.shape["dp"] // 2
    ny = nx if mesh.shape["tm"] % nx == 0 else 1
    nz = mesh.shape["tm"] // ny
    return jax.shard_map(
        functools.partial(shards, nz, ny, nx),
        mesh=mesh,
        in_specs=(P("dp", "tm", None), P(), P("dp", "tm", None)),
        out_specs=(P("dp", "tm", None), P("tm", None)),
        check_vma=False,
    )
```

time: 326 us -> 81.6 us (0.25)
  waiting for transfers between devices: 201 us -> 0 us
  Pallas kernels: 0 us -> 76.2 us
  matrix products: 44.4 us -> 0 us
  local copies, waits for them, and re-layouts: 37.1 us -> 4.04 us
  other arithmetic: 28.2 us -> 0 us
  between operations: 13.9 us -> 0.65 us
    reduce_scatter x1 -> x0, waiting for transfers between devices: 117 us -> none  [shards(): lax.psum_scatter(lax.dot_general(record, dqkv, (((0,), (0,)), ((), ())),...]
    pallas_call x0 -> x1, Pallas kernels: none -> 76.2 us  [shards(): pl.pallas_call(functools.partial(kernel, (nz, ny, nx)), out_shape=(jax.Sh...]
    all_gather x2 -> x0, waiting for transfers between devices: 54.5 us -> none  [carried_in(): pieces = lax.all_gather(value, axis)]
    dot_general x12 -> x0, matrix products: 44.4 us -> none  [the longest x1 7.36 us: shards(): lax.dot_general(record, dqkv, (((0,), (0,)), ((), ())), preferred_element...]
    psum x1 -> x0, waiting for transfers between devices: 29.5 us -> none  [shards(): proj_grad = lax.psum(partial_rows, 'dp')]
    select_n x14 -> x0, other arithmetic: 19.6 us -> none  [lap(): return jnp.where(position < mine, longer, so_far)]
    add x3 -> x0, local copies, waits for them, and re-layouts: 7.04 us -> none  [the longest x1 2.35 us: shards(): jnp.einsum('nhts,nthd->nshd', mix_vg, queries, preferred_element_type=f32)]
    reshape x3 -> x0, local copies, waits for them, and re-layouts: 6.57 us -> none  [the longest x1 2.24 us: shards(): queries = qkv[:, :width].reshape(shape4)]
  transfers between devices with their start and end apart: 4 -> 0, of which waited for: 4 -> 0; matrix products, arithmetic and copies ran while one was open for 16% -> 0% of each run, Pallas kernels for 0% -> 0%
where the time goes in v1:
time: 81.6 us; the launch traced here: 80.8 us
  Pallas kernels  76.2 us (93%)
  local copies, waits for them, and re-layouts  4.04 us (5%)
    pallas_call x1, Pallas kernels, shards(): pl.pallas_call(functools.partial(kernel, (nz, ny, nx)), out_shape=(jax.Sh...  76.2 us
    unnamed x4, local copies, waits for them, and re-layouts  4.04 us

profile of v1, /device:TPU:0, one launch (start us, length us, event | category | flops | bytes accessed | tf_op | source)
XLA Modules:
  0.0 80.8 jit_solution(1969206964275801339)
XLA Ops:
  0.6 76.2 %shard_map.50 = (bf16[1024,1024]{1,0:T(8,128)(2,1)}, f32[128,1536]{1,0:T(8,128)}) custom-call(bf16[1024,1024]{1,0:T(8,128)(2,1)} %bitcast.3, bf16[1024,1536]{1,0:T(8,128)(2,1)} %w_ref.1, bf16[1024,512]{1,0:T(8,128)(2,1)} %bitcast.5), custom_call_target="tpu_custom_call" | custom-call | tf_op jit(solution)/shard_map/pallas_call | solution.py:433
  76.8 0.0 copy-start
  76.8 3.2 %copy.7 = bf16[1,1024,1024]{2,1,0:T(8,128)(2,1)} copy(bf16[1,1024,1024]{2,1,0:T(8,128)(2,1)} %bitcast.4) | data formatting | bytes 4194304
  80.0 0.0 copy-done
  80.0 0.9 %copy.8 = f32[128,1536]{1,0:T(8,128)} copy(f32[128,1536]{1,0:T(8,128)S(1)} %copy-done) | data formatting | bytes 1572864
Async XLA Ops:
  76.8 3.2 %copy-start = (f32[128,1536]{1,0:T(8,128)S(1)}, f32[128,1536]{1,0:T(8,128)}, u32[]{:S(2)}) copy-start(f32[128,1536]{1,0:T(8,128)} %get-tuple-element.9) | copy-start | bytes 2359300

commit v2 on v1

v2 whole, which is shorter than its diff:
```python
import functools

import jax
import jax.numpy as jnp
from jax import lax
from jax.experimental import pallas as pl
from jax.experimental.pallas import tpu as pltpu
from jax.sharding import PartitionSpec as P

H = 4
HD = 128
CH = 256
MESH = pl.DeviceIdType.MESH
F32 = jnp.float32
BF16 = jnp.bfloat16
NN = (((1,), (0,)), ((), ()))
NT = (((1,), (1,)), ((), ()))
TN = (((0,), (0,)), ((), ()))


def mm(a, b, dims=NN):
    return lax.dot_general(a, b, dims, preferred_element_type=F32)


FIRST = ((0, 0), (0, 1), (0, 2), (1, 0))
SECOND = ((1, 1), (1, 2))


def kernel(
    sizes,
    x_ref, w_ref, og_ref, dx_ref, dw_ref,
    qkv, sc, kvg, qgg, loc, dqkv, xt, dxs, dx_sem,
    kst, qst, kyr, qyr,
    part, crecv, a_xr, a_yr, a2, a_zr, ga, b_yr, b_zr, b2, b_xr, b3, gb,
    zk_s, zk_r, zq_s, zq_r, yk_s, yk_r, yq_s, yq_r,
    c_s, c_r, ax_s, ax_r, ay_s, ay_r, az_s, az_r, ag_s, ag_r,
    by_s, by_r, bz_s, bz_r, bx_s, bx_r, gb_s, gb_r,
):
    nz, ny, nx = sizes
    tok = x_ref.shape[0]
    nb = tok // CH
    width = H * HD
    rx = dw_ref.shape[0] // nx
    dm = x_ref.shape[1]
    tm, dp = lax.axis_index("tm"), lax.axis_index("dp")
    z, y = tm // ny, lax.rem(tm, ny)
    x, c = dp // 2, lax.rem(dp, 2)

    def at(z_=None, y_=None, x_=None, c_=None):
        z_ = z if z_ is None else z_
        y_ = y if y_ is None else y_
        x_ = x if x_ is None else x_
        c_ = c if c_ is None else c_
        return (z_ * ny + y_, x_ * 2 + c_)

    def zpeer(d):
        return lax.rem(z + d, nz)

    def ypeer(d):
        return lax.rem(y + d, ny)

    def xpeer(d):
        return lax.rem(x + d, nx)

    def remote(src, dst, send, recv, device):
        return pltpu.make_async_remote_copy(
            src_ref=src, dst_ref=dst, send_sem=send, recv_sem=recv,
            device_id=device, device_id_type=MESH,
        )

    def head(p):
        return 2 * lax.rem(p + 1 - c, 2) + p // 2

    peers = [at(c_=1 - c)]
    for d in range(1, nx):
        peers += [at(x_=xpeer(d)), at(x_=xpeer(d), c_=1 - c)]
    peers += [at(y_=ypeer(d)) for d in range(1, ny)]
    peers += [at(z_=zpeer(d)) for d in range(1, nz)]
    barrier = pltpu.get_barrier_semaphore()
    for peer in peers:
        pl.semaphore_signal(barrier, inc=1, device_id=peer, device_id_type=MESH)

    def project(n, carry):
        rows = pl.ds(pl.multiple_of(n * CH, CH), CH)
        r = mm(x_ref[rows, :], w_ref[...]).astype(BF16)
        pos = tm * tok + n * CH + lax.broadcasted_iota(jnp.int32, (CH, 1), 0)
        factor = 1.0 / jnp.sqrt(jnp.float32(HD) * (pos.astype(F32) + 1.0))
        g = (og_ref[rows, :].astype(F32) * factor).astype(BF16)
        for h in range(H):
            q = r[:, h * HD : (h + 1) * HD]
            k = r[:, width + h * HD : width + (h + 1) * HD]
            v = r[:, 2 * width + h * HD : 2 * width + (h + 1) * HD]
            s = g[:, h * HD : (h + 1) * HD]
            qkv[0, h, rows, :] = q
            qkv[1, h, rows, :] = k
            qkv[2, h, rows, :] = v
            sc[h, rows, :] = s
            kvg[n, h] = mm(k, v, TN)
            qgg[n, h] = mm(q, s, TN)
        return carry

    lax.fori_loop(0, nb, project, 0)

    pl.semaphore_wait(barrier, len(peers))

    @pl.when(z == 0)
    def _():
        kst[0] = jnp.zeros_like(kst[0])

    @pl.when(z == nz - 1)
    def _():
        qst[0] = jnp.zeros_like(qst[0])

    def link(p, ord_, last, nxt, st, grp, zs, zr, ys, yr_, ybuf, later):
        @pl.when(ord_ > 0)
        def _():
            remote(st.at[1, p], st.at[0, p], zs.at[p], zr.at[p], at(z_=z)).wait_recv()

        hh = head(p)
        total = st[0, p]
        for n in range(nb):
            total = total + grp[n, hh]
        st[1, p] = total

        @pl.when(ord_ < nz - 1)
        def _():
            remote(st.at[1, p], st.at[0, p], zs.at[p], zr.at[p], at(z_=nxt)).start()

        for d in range(1, ny):
            other = ypeer(d)
            which = jnp.where(later(other), 1, 0)
            remote(
                st.at[which, p], ybuf.at[d - 1, p], ys.at[d - 1, p], yr_.at[d - 1, p],
                at(y_=other),
            ).start()

    def local(n, p):
        hh = head(p)
        rows = pl.ds(pl.multiple_of(n * CH, CH), CH)
        q, k, v, s = qkv[0, hh, rows, :], qkv[1, hh, rows, :], qkv[2, hh, rows, :], sc[hh, rows, :]
        row = lax.broadcasted_iota(jnp.int32, (CH, CH), 0)
        col = lax.broadcasted_iota(jnp.int32, (CH, CH), 1)
        low, up = row >= col, row <= col
        vg = jnp.where(low, mm(s, v, NT), 0.0).astype(BF16)
        vgt = jnp.where(up, mm(v, s, NT), 0.0).astype(BF16)
        qkt = jnp.where(up, mm(k, q, NT), 0.0).astype(BF16)
        loc[0, p, rows, :] = mm(vg, k)
        loc[1, p, rows, :] = mm(vgt, q)
        loc[2, p, rows, :] = mm(qkt, s)

    def core_copy(slot, j):
        return remote(part.at[2 * slot, j], crecv.at[slot, j], c_s.at[slot, j], c_r.at[slot, j], at(c_=1 - c))

    def mine(g):
        return part.at[2 * g[0] + 1, g[1]]

    def ax_copy(d, a):
        o = xpeer(d)
        return remote(
            mine(FIRST[a]).at[:, :, o], a_xr.at[d - 1, a], ax_s.at[d - 1, a], ax_r.at[d - 1, a], at(x_=o)
        )

    def ay_copy(d, a):
        o = ypeer(d)
        return remote(
            mine(FIRST[a]).at[:, o, x], a_yr.at[d - 1, a], ay_s.at[d - 1, a], ay_r.at[d - 1, a], at(y_=o)
        )

    def az_copy(d, a):
        o = zpeer(d)
        return remote(a2.at[a, o], a_zr.at[d - 1, a], az_s.at[d - 1, a], az_r.at[d - 1, a], at(z_=o))

    def by_copy(d, b):
        o = ypeer(d)
        return remote(
            mine(SECOND[b]).at[:, o], b_yr.at[d - 1, b], by_s.at[d - 1, b], by_r.at[d - 1, b], at(y_=o)
        )

    def bz_copy(d, b):
        o = zpeer(d)
        return remote(
            mine(SECOND[b]).at[o, y], b_zr.at[d - 1, b], bz_s.at[d - 1, b], bz_r.at[d - 1, b], at(z_=o)
        )

    def bx_copy(d, b):
        o = xpeer(d)
        return remote(b2.at[b], b_xr.at[d - 1, b], bx_s.at[d - 1, b], bx_r.at[d - 1, b], at(x_=o))

    def gb_copy(b):
        return remote(b3.at[b], gb.at[b], gb_s.at[b], gb_r.at[b], at(c_=1 - c))

    def ag_copy(e, j):
        d, flip = e // 2, e % 2
        o = xpeer(d)
        oc = 1 - c if flip else c
        return remote(ga.at[0, j], ga.at[e, j], ag_s.at[e, j], ag_r.at[e, j], at(x_=o, c_=oc))

    def finish(p):
        hh = head(p)
        start, end = kst[0, p], qst[0, p]
        for d in range(1, ny):
            remote(kst.at[0, p], kyr.at[d - 1, p], yk_s.at[d - 1, p], yk_r.at[d - 1, p], at(y_=ypeer(d))).wait_recv()
            remote(qst.at[0, p], qyr.at[d - 1, p], yq_s.at[d - 1, p], yq_r.at[d - 1, p], at(y_=ypeer(d))).wait_recv()
            start = start + kyr[d - 1, p]
            end = end + qyr[d - 1, p]
        cols = [pl.ds(pl.multiple_of(j * width + hh * HD, HD), HD) for j in range(3)]
        for n in range(nb):
            rows = pl.ds(n * CH, CH)
            dq = loc[0, p, rows, :] + mm(sc[hh, rows, :], start.astype(BF16), NT)
            dqkv[rows, cols[0]] = dq.astype(BF16)
            start = start + kvg[n, hh]
        for n in range(nb - 1, -1, -1):
            rows = pl.ds(n * CH, CH)
            after = end.astype(BF16)
            dk = loc[1, p, rows, :] + mm(qkv[2, hh, rows, :], after, NT)
            dv = loc[2, p, rows, :] + mm(qkv[1, hh, rows, :], after)
            dqkv[rows, cols[1]] = dk.astype(BF16)
            dqkv[rows, cols[2]] = dv.astype(BF16)
            end = end + qgg[n, hh]
        d = jnp.concatenate([dqkv[:, cols[j]] for j in range(3)], axis=1)
        zrows = dm // nz

        def slab(i, carry):
            rows = pl.ds(pl.multiple_of(i * zrows, zrows), zrows)
            r = mm(xt[rows, :], d)
            for j in range(3):
                part[p, j, i] = r[:, j * HD : (j + 1) * HD].reshape(ny, nx, rx, HD)
            return carry

        lax.fori_loop(0, nz, slab, 0)

    def head_step(p):
        finish(p)
        slot = p // 2

        @pl.when(lax.rem(p, 2) == 0)
        def _():
            for j in range(3):
                core_copy(slot, j).start()

        @pl.when(lax.rem(p, 2) == 1)
        def _():
            for j in range(3):
                core_copy(slot, j).wait_recv()
                for i in range(nz):
                    part[p, j, i] = part[p, j, i] + crecv[slot, j, i]
                for s_ in range(2):

                    @pl.when(slot == s_)
                    def _():
                        if (s_, j) in FIRST:
                            for d in range(1, nx):
                                ax_copy(d, FIRST.index((s_, j))).start()
                        else:
                            for d in range(1, ny):
                                by_copy(d, SECOND.index((s_, j))).start()

    items = nb * (H + 1)
    per = 1
    while any((nz + p + 1) * per < nb * (p + 2) for p in range(H)):
        per += 1

    def step(i, carry):
        kp = i - z
        qp = i - (nz - 1 - z)

        @pl.when((kp >= 0) & (kp < H))
        def _():
            link(kp, z, nz, z + 1, kst, kvg, zk_s, zk_r, yk_s, yk_r, kyr, lambda o: o > y)

        @pl.when((qp >= 0) & (qp < H))
        def _():
            link(qp, nz - 1 - z, nz, z - 1, qst, qgg, zq_s, zq_r, yq_s, yq_r, qyr, lambda o: o < y)

        def piece(u, carry):
            idx = i * per + u
            group, n = idx // nb, lax.rem(idx, nb)

            @pl.when((idx < items) & (group != 1))
            def _():
                local(n, jnp.where(group == 0, 0, group - 1))

            @pl.when(group == 1)
            def _():
                rows = pl.ds(pl.multiple_of(n * CH, CH), CH)
                xt[:, rows] = x_ref[rows, :].T

            return carry

        lax.fori_loop(0, per, piece, 0)

        @pl.when(i >= nz)
        def _():
            head_step(i - nz)

        return carry

    lax.fori_loop(0, nz + H, step, 0)

    def out_copy(i):
        rows = pl.ds(i * CH, CH)
        return pltpu.make_async_copy(dxs.at[rows, :], dx_ref.at[rows, :], dx_sem.at[i])

    def rows_of(i):
        rows = pl.ds(i * CH, CH)
        dxs[rows, :] = mm(dqkv[rows, :], w_ref[...], NT)
        out_copy(i).start()

    def a_one(a):
        for d in range(1, nx):
            ax_copy(d, a).wait_recv()
        own = mine(FIRST[a])
        for i in range(nz):
            t = own[i, :, x]
            for d in range(1, nx):
                t = t + a_xr[d - 1, a, i]
            own[i, :, x] = t
        for d in range(1, ny):
            ay_copy(d, a).start()

    def a_two(a):
        for d in range(1, ny):
            ay_copy(d, a).wait_recv()
        own = mine(FIRST[a])
        for i in range(nz):
            t = own[i, y, x]
            for d in range(1, ny):
                t = t + a_yr[d - 1, a, i]
            a2[a, i] = t
        for d in range(1, nz):
            az_copy(d, a).start()

    def a_three(a):
        for d in range(1, nz):
            az_copy(d, a).wait_recv()
        t = a2[a, z]
        for d in range(1, nz):
            t = t + a_zr[d - 1, a]
        ga[0, a] = t
        for e in range(1, 2 * nx):
            ag_copy(e, a).start()

    def cols_of(g, core):
        return pl.ds(pl.multiple_of(g[1] * width + (2 * core + g[0]) * HD, HD), HD)

    def a_last(a):
        for e in range(2 * nx):
            if e:
                ag_copy(e, a).wait_recv()
            d, flip = e // 2, e % 2
            o = lax.rem(x - d + nx, nx)
            rows = pl.ds(pl.multiple_of(o * rx, rx), rx)
            dw_ref[rows, cols_of(FIRST[a], 1 - c if flip else c)] = ga[e, a]

    def b_one(b):
        for d in range(1, ny):
            by_copy(d, b).wait_recv()
        own = mine(SECOND[b])
        for i in range(nz):
            t = own[i, y]
            for d in range(1, ny):
                t = t + b_yr[d - 1, b, i]
            own[i, y] = t
        for d in range(1, nz):
            bz_copy(d, b).start()

    def b_two(b):
        for d in range(1, nz):
            bz_copy(d, b).wait_recv()
        t = mine(SECOND[b])[z, y]
        for d in range(1, nz):
            t = t + b_zr[d - 1, b]
        b2[b] = t
        for d in range(1, nx):
            bx_copy(d, b).start()

    def b_three(b):
        for d in range(1, nx):
            bx_copy(d, b).wait_recv()
        t = b2[b]
        for d in range(1, nx):
            t = t + b_xr[d - 1, b]
        b3[b] = t
        gb_copy(b).start()
        dw_ref[:, cols_of(SECOND[b], c)] = t.reshape(nx * rx, HD)

    def b_last(b):
        gb_copy(b).wait_recv()
        dw_ref[:, cols_of(SECOND[b], 1 - c)] = gb[b].reshape(nx * rx, HD)

    order = [
        (a_one, 0), (rows_of, 0), (b_one, 0), (rows_of, 1), (a_one, 1), (rows_of, 2), (a_two, 0),
        (rows_of, 3), (b_one, 1), (b_two, 0), (a_one, 2), (a_two, 1), (a_three, 0), (b_three, 0),
        (a_one, 3), (a_two, 2), (b_two, 1), (a_three, 1), (b_three, 1), (a_two, 3), (a_three, 2),
        (a_three, 3), (b_last, 0), (b_last, 1), (a_last, 0), (a_last, 1), (a_last, 2), (a_last, 3),
    ]
    for work, i in order:
        work(i)
    for i in range(nb):
        out_copy(i).wait()

    def drain_state(p, carry):
        @pl.when(z < nz - 1)
        def _():
            remote(kst.at[1, p], kst.at[0, p], zk_s.at[p], zk_r.at[p], at(z_=z)).wait_send()

        @pl.when(z > 0)
        def _():
            remote(qst.at[1, p], qst.at[0, p], zq_s.at[p], zq_r.at[p], at(z_=z)).wait_send()

        for d in range(1, ny):
            remote(kst.at[0, p], kyr.at[d - 1, p], yk_s.at[d - 1, p], yk_r.at[d - 1, p], at(y_=ypeer(d))).wait_send()
            remote(qst.at[0, p], qyr.at[d - 1, p], yq_s.at[d - 1, p], yq_r.at[d - 1, p], at(y_=ypeer(d))).wait_send()
        return carry

    lax.fori_loop(0, H, drain_state, 0)
    for j in range(3):
        core_copy(0, j).wait_send()
        core_copy(1, j).wait_send()
    for a in range(len(FIRST)):
        for d in range(1, nx):
            ax_copy(d, a).wait_send()
        for d in range(1, ny):
            ay_copy(d, a).wait_send()
        for d in range(1, nz):
            az_copy(d, a).wait_send()
        for e in range(1, 2 * nx):
            ag_copy(e, a).wait_send()
    for b in range(len(SECOND)):
        for d in range(1, ny):
            by_copy(d, b).wait_send()
        for d in range(1, nz):
            bz_copy(d, b).wait_send()
        for d in range(1, nx):
            bx_copy(d, b).wait_send()
        gb_copy(b).wait_send()


def shards(nz, ny, nx, inputs, weights, out_grad):
    record, cot = inputs[0], out_grad[0]
    tok, dm = record.shape
    nb = tok // CH
    rx = dm // (nz * ny * nx)
    na, ns = len(FIRST), len(SECOND)
    V = pltpu.VMEM
    D = pltpu.SemaphoreType.DMA
    scratch = [
        V((3, H, tok, HD), BF16), V((H, tok, HD), BF16),
        V((nb, H, HD, HD), F32), V((nb, H, HD, HD), F32),
        V((3, H, tok, HD), F32), V((tok, 3 * H * HD), BF16), V((dm, tok), BF16),
        V((tok, dm), F32), D((nb,)),
        V((2, H, HD, HD), F32), V((2, H, HD, HD), F32),
        V((ny - 1, H, HD, HD), F32), V((ny - 1, H, HD, HD), F32),
        V((4, 3, nz, ny, nx, rx, HD), F32), V((2, 3, nz, ny, nx, rx, HD), F32),
        V((nx - 1, na, nz, ny, rx, HD), F32), V((ny - 1, na, nz, rx, HD), F32),
        V((na, nz, rx, HD), F32), V((nz - 1, na, rx, HD), F32), V((2 * nx, na, rx, HD), F32),
        V((ny - 1, ns, nz, nx, rx, HD), F32), V((nz - 1, ns, nx, rx, HD), F32),
        V((ns, nx, rx, HD), F32), V((nx - 1, ns, nx, rx, HD), F32),
        V((ns, nx, rx, HD), F32), V((ns, nx, rx, HD), F32),
        D((H,)), D((H,)), D((H,)), D((H,)),
        D((ny - 1, H)), D((ny - 1, H)), D((ny - 1, H)), D((ny - 1, H)),
        D((2, 3)), D((2, 3)), D((nx - 1, na)), D((nx - 1, na)), D((ny - 1, na)), D((ny - 1, na)),
        D((nz - 1, na)), D((nz - 1, na)), D((2 * nx, na)), D((2 * nx, na)),
        D((ny - 1, ns)), D((ny - 1, ns)), D((nz - 1, ns)), D((nz - 1, ns)),
        D((nx - 1, ns)), D((nx - 1, ns)), D((ns,)), D((ns,)),
    ]
    vm = pl.BlockSpec(memory_space=pltpu.VMEM)
    dx, dw = pl.pallas_call(
        functools.partial(kernel, (nz, ny, nx)),
        out_shape=(
            jax.ShapeDtypeStruct((tok, dm), F32),
            jax.ShapeDtypeStruct((dm // (nz * ny), weights.shape[1]), F32),
        ),
        in_specs=[vm, vm, vm],
        out_specs=(pl.BlockSpec(memory_space=pl.ANY), vm),
        scratch_shapes=scratch,
        compiler_params=pltpu.CompilerParams(
            collective_id=0, has_side_effects=True, vmem_limit_bytes=60 * 1024 * 1024
        ),
    )(record, weights, cot)
    return dx.astype(BF16)[None], dw


def solution(mesh):
    nx = mesh.shape["dp"] // 2
    ny = nx if mesh.shape["tm"] % nx == 0 else 1
    nz = mesh.shape["tm"] // ny
    return jax.shard_map(
        functools.partial(shards, nz, ny, nx),
        mesh=mesh,
        in_specs=(P("dp", "tm", None), P(), P("dp", "tm", None)),
        out_specs=(P("dp", "tm", None), P("tm", None)),
        check_vma=False,
    )
```

time: 81.6 us -> 84.5 us (1.036)
  other arithmetic: 0 us -> 3.91 us
  local copies, waits for them, and re-layouts: 4.04 us -> 0.88 us
  Pallas kernels: 76.2 us -> 78.9 us
    broadcast_in_dim x0 -> x1, other arithmetic: none -> 3.91 us  [shards(): return (dx.astype(BF16)[None], dw)]
    unnamed x4 -> x3, local copies, waits for them, and re-layouts: 4.04 us -> 0.88 us
    pallas_call x1, Pallas kernels: 76.2 us -> 78.9 us  [shards(): pl.pallas_call(functools.partial(kernel, (nz, ny, nx)), out_shape=(jax.Sh...]
where the time goes in v2:
time: 84.5 us; the launch traced here: 84.4 us
  Pallas kernels  78.9 us (93%)
  other arithmetic  3.91 us (5%)
  local copies, waits for them, and re-layouts  0.88 us (1%)
    pallas_call x1, Pallas kernels, shards(): pl.pallas_call(functools.partial(kernel, (nz, ny, nx)), out_shape=(jax.Sh...  78.9 us
    broadcast_in_dim x1, other arithmetic, shards(): return (dx.astype(BF16)[None], dw)  3.91 us

profile of v2, /device:TPU:0, one launch (start us, length us, event | category | flops | bytes accessed | tf_op | source)
XLA Modules:
  0.0 84.4 jit_solution(4058596925437034139)
XLA Ops:
  0.6 78.9 %shard_map.50 = (f32[1024,1024]{1,0:T(8,128)}, f32[128,1536]{1,0:T(8,128)}) custom-call(bf16[1024,1024]{1,0:T(8,128)(2,1)} %bitcast.4, bf16[1024,1536]{1,0:T(8,128)(2,1)} %w_ref.1, bf16[1024,512]{1,0:T(8,128)(2,1)} %bitcast.5), custom_call_target="tpu_custom_call" | custom-call | tf_op jit(solution)/shard_map/pallas_call | solution.py:468
  79.6 0.0 copy-start
  79.6 3.9 %convert_bitcast_fusion = bf16[1,1024,1024]{2,1,0:T(8,128)(2,1)} fusion(f32[1024,1024]{1,0:T(8,128)} %get-tuple-element.4), kind=kLoop, calls=%fused_computation | loop fusion | flops 1048576 | bytes 6291456 | tf_op jit(solution)/shard_map/broadcast_in_dim | solution.py:481
  83.5 0.0 copy-done
  83.5 0.9 %copy.6 = f32[128,1536]{1,0:T(8,128)} copy(f32[128,1536]{1,0:T(8,128)S(1)} %copy-done) | data formatting | bytes 1572864
Async XLA Ops:
  79.6 3.9 %copy-start = (f32[128,1536]{1,0:T(8,128)S(1)}, f32[128,1536]{1,0:T(8,128)}, u32[]{:S(2)}) copy-start(f32[128,1536]{1,0:T(8,128)} %get-tuple-element.9) | copy-start | bytes 2359300

commit v3 on v2

--- a/solution.py
+++ b/solution.py
@@ -22,18 +22,18 @@
     return lax.dot_general(a, b, dims, preferred_element_type=F32)
 
 
-FIRST = ((0, 0), (0, 1), (0, 2), (1, 0))
-SECOND = ((1, 1), (1, 2))
+FIRST = ((0, 0), (0, 1), (0, 2))
+SECOND = ((1, 0), (1, 1), (1, 2))
 
 
 def kernel(
     sizes,
-    x_ref, w_ref, og_ref, dx_ref, dw_ref,
-    qkv, sc, kvg, qgg, loc, dqkv, xt, dxs, dx_sem,
+    x_hbm, w_hbm, og_hbm, dx_ref, dw_ref,
+    x_ref, w_ref, og_ref, in_sem, dcat, qkv, sc, kvg, qgg, loc, dqkv, xt, dxs, dx_sem,
     kst, qst, kyr, qyr,
     part, crecv, a_xr, a_yr, a2, a_zr, ga, b_yr, b_zr, b2, b_xr, b3, gb,
     zk_s, zk_r, zq_s, zq_r, yk_s, yk_r, yq_s, yq_r,
-    c_s, c_r, ax_s, ax_r, ay_s, ay_r, az_s, az_r, ag_s, ag_r,
+    c_s, c_r, ax_s, ax_r, ay_s, ay_r, az_s, az_r, ag_s, ag_r, af_s, af_r,
     by_s, by_r, bz_s, bz_r, bx_s, bx_r, gb_s, gb_r,
 ):
     nz, ny, nx = sizes
@@ -73,33 +73,52 @@
 
     peers = [at(c_=1 - c)]
     for d in range(1, nx):
-        peers += [at(x_=xpeer(d)), at(x_=xpeer(d), c_=1 - c)]
+        peers += [at(x_=xpeer(d))]
     peers += [at(y_=ypeer(d)) for d in range(1, ny)]
     peers += [at(z_=zpeer(d)) for d in range(1, nz)]
     barrier = pltpu.get_barrier_semaphore()
     for peer in peers:
         pl.semaphore_signal(barrier, inc=1, device_id=peer, device_id_type=MESH)
 
-    def project(n, carry):
+    tile = 2 * HD
+    tiles = 3 * width // tile
+
+    def weight_copy(i):
+        cols = pl.ds(pl.multiple_of(i * tile, tile), tile)
+        return pltpu.make_async_copy(w_hbm.at[:, cols], w_ref.at[:, cols], in_sem.at[i])
+
+    x_copy = pltpu.make_async_copy(x_hbm, x_ref, in_sem.at[tiles])
+    og_copy = pltpu.make_async_copy(og_hbm, og_ref, in_sem.at[tiles + 1])
+    x_copy.start()
+    for i in range(tiles):
+        weight_copy(i).start()
+    og_copy.start()
+    x_copy.wait()
+
+    def project(i, carry):
+        weight_copy(i).wait()
+        r = mm(x_ref[...], w_ref[:, pl.ds(pl.multiple_of(i * tile, tile), tile)]).astype(BF16)
+        j, pair = i // (H // 2), lax.rem(i, H // 2)
+        qkv[j, 2 * pair] = r[:, :HD]
+        qkv[j, 2 * pair + 1] = r[:, HD:]
+        return carry
+
+    lax.fori_loop(0, tiles, project, 0)
+    og_copy.wait()
+
+    def sums(n, carry):
         rows = pl.ds(pl.multiple_of(n * CH, CH), CH)
-        r = mm(x_ref[rows, :], w_ref[...]).astype(BF16)
         pos = tm * tok + n * CH + lax.broadcasted_iota(jnp.int32, (CH, 1), 0)
         factor = 1.0 / jnp.sqrt(jnp.float32(HD) * (pos.astype(F32) + 1.0))
         g = (og_ref[rows, :].astype(F32) * factor).astype(BF16)
         for h in range(H):
-            q = r[:, h * HD : (h + 1) * HD]
-            k = r[:, width + h * HD : width + (h + 1) * HD]
-            v = r[:, 2 * width + h * HD : 2 * width + (h + 1) * HD]
-            s = g[:, h * HD : (h + 1) * HD]
-            qkv[0, h, rows, :] = q
-            qkv[1, h, rows, :] = k
-            qkv[2, h, rows, :] = v
-            sc[h, rows, :] = s
-            kvg[n, h] = mm(k, v, TN)
-            qgg[n, h] = mm(q, s, TN)
+            sg = g[:, h * HD : (h + 1) * HD]
+            sc[h, rows, :] = sg
+            kvg[n, h] = mm(qkv[1, h, rows, :], qkv[2, h, rows, :], TN)
+            qgg[n, h] = mm(qkv[0, h, rows, :], sg, TN)
         return carry
 
-    lax.fori_loop(0, nb, project, 0)
+    lax.fori_loop(0, nb, sums, 0)
 
     pl.semaphore_wait(barrier, len(peers))
 
@@ -189,11 +208,13 @@
     def gb_copy(b):
         return remote(b3.at[b], gb.at[b], gb_s.at[b], gb_r.at[b], at(c_=1 - c))
 
-    def ag_copy(e, j):
-        d, flip = e // 2, e % 2
-        o = xpeer(d)
-        oc = 1 - c if flip else c
-        return remote(ga.at[0, j], ga.at[e, j], ag_s.at[e, j], ag_r.at[e, j], at(x_=o, c_=oc))
+    def ag_copy(d, a):
+        return remote(
+            ga.at[0, 0, a], ga.at[0, d, a], ag_s.at[d - 1, a], ag_r.at[d - 1, a], at(x_=xpeer(d))
+        )
+
+    def af_copy(d, a):
+        return remote(ga.at[0, d, a], ga.at[1, d, a], af_s.at[d, a], af_r.at[d, a], at(c_=1 - c))
 
     def finish(p):
         hh = head(p)
@@ -208,6 +229,7 @@
             rows = pl.ds(n * CH, CH)
             dq = loc[0, p, rows, :] + mm(sc[hh, rows, :], start.astype(BF16), NT)
             dqkv[rows, cols[0]] = dq.astype(BF16)
+            dcat[rows, :HD] = dq.astype(BF16)
             start = start + kvg[n, hh]
         for n in range(nb - 1, -1, -1):
             rows = pl.ds(n * CH, CH)
@@ -216,18 +238,20 @@
             dv = loc[2, p, rows, :] + mm(qkv[1, hh, rows, :], after)
             dqkv[rows, cols[1]] = dk.astype(BF16)
             dqkv[rows, cols[2]] = dv.astype(BF16)
+            dcat[rows, HD : 2 * HD] = dk.astype(BF16)
+            dcat[rows, 2 * HD :] = dv.astype(BF16)
             end = end + qgg[n, hh]
-        d = jnp.concatenate([dqkv[:, cols[j]] for j in range(3)], axis=1)
-        zrows = dm // nz
+        zb = 2 if nz % 2 == 0 else 1
+        m = zb * (dm // nz)
 
         def slab(i, carry):
-            rows = pl.ds(pl.multiple_of(i * zrows, zrows), zrows)
-            r = mm(xt[rows, :], d)
+            rows = pl.ds(pl.multiple_of(i * m, m), m)
+            r = mm(xt[rows, :], dcat[...])
             for j in range(3):
-                part[p, j, i] = r[:, j * HD : (j + 1) * HD].reshape(ny, nx, rx, HD)
+                part[p, j, pl.ds(i * zb, zb)] = r[:, j * HD : (j + 1) * HD].reshape(zb, ny, nx, rx, HD)
             return carry
 
-        lax.fori_loop(0, nz, slab, 0)
+        lax.fori_loop(0, nz // zb, slab, 0)
 
     def head_step(p):
         finish(p)
@@ -297,14 +321,13 @@
 
     lax.fori_loop(0, nz + H, step, 0)
 
-    def out_copy(i):
-        rows = pl.ds(i * CH, CH)
-        return pltpu.make_async_copy(dxs.at[rows, :], dx_ref.at[rows, :], dx_sem.at[i])
+    out_copy = pltpu.make_async_copy(dxs, dx_ref, dx_sem)
 
     def rows_of(i):
-        rows = pl.ds(i * CH, CH)
-        dxs[rows, :] = mm(dqkv[rows, :], w_ref[...], NT)
-        out_copy(i).start()
+        cols = pl.ds(i * tile, tile)
+        dxs[:, cols] = mm(dqkv[...], w_ref[cols, :], NT).astype(BF16)
+        if (i + 1) * tile == dm:
+            out_copy.start()
 
     def a_one(a):
         for d in range(1, nx):
@@ -336,21 +359,29 @@
         t = a2[a, z]
         for d in range(1, nz):
             t = t + a_zr[d - 1, a]
-        ga[0, a] = t
-        for e in range(1, 2 * nx):
-            ag_copy(e, a).start()
+        ga[0, 0, a] = t
+        for d in range(1, nx):
+            ag_copy(d, a).start()
+        af_copy(0, a).start()
 
     def cols_of(g, core):
         return pl.ds(pl.multiple_of(g[1] * width + (2 * core + g[0]) * HD, HD), HD)
 
+    def place(flip, d, a):
+        rows = pl.ds(pl.multiple_of(lax.rem(x - d + nx, nx) * rx, rx), rx)
+        dw_ref[rows, cols_of(FIRST[a], 1 - c if flip else c)] = ga[flip, d, a]
+
+    def a_four(a):
+        for d in range(1, nx):
+            ag_copy(d, a).wait_recv()
+            af_copy(d, a).start()
+        for d in range(nx):
+            place(0, d, a)
+
     def a_last(a):
-        for e in range(2 * nx):
-            if e:
-                ag_copy(e, a).wait_recv()
-            d, flip = e // 2, e % 2
-            o = lax.rem(x - d + nx, nx)
-            rows = pl.ds(pl.multiple_of(o * rx, rx), rx)
-            dw_ref[rows, cols_of(FIRST[a], 1 - c if flip else c)] = ga[e, a]
+        for d in range(nx):
+            af_copy(d, a).wait_recv()
+            place(1, d, a)
 
     def b_one(b):
         for d in range(1, ny):
@@ -388,16 +419,16 @@
         gb_copy(b).wait_recv()
         dw_ref[:, cols_of(SECOND[b], 1 - c)] = gb[b].reshape(nx * rx, HD)
 
-    order = [
-        (a_one, 0), (rows_of, 0), (b_one, 0), (rows_of, 1), (a_one, 1), (rows_of, 2), (a_two, 0),
-        (rows_of, 3), (b_one, 1), (b_two, 0), (a_one, 2), (a_two, 1), (a_three, 0), (b_three, 0),
-        (a_one, 3), (a_two, 2), (b_two, 1), (a_three, 1), (b_three, 1), (a_two, 3), (a_three, 2),
-        (a_three, 3), (b_last, 0), (b_last, 1), (a_last, 0), (a_last, 1), (a_last, 2), (a_last, 3),
+    order = [(a_one, 0)] + [(rows_of, i) for i in range(dm // tile)]
+    order += [
+        (a_one, 1), (b_one, 0), (a_one, 2), (a_two, 0), (b_one, 1), (a_two, 1), (b_two, 0),
+        (b_one, 2), (a_two, 2), (b_two, 1), (b_three, 0), (a_three, 0), (b_two, 2), (b_three, 1),
+        (a_three, 1), (a_four, 0), (a_three, 2), (b_three, 2), (a_four, 1), (a_four, 2),
+        (b_last, 0), (b_last, 1), (b_last, 2), (a_last, 0), (a_last, 1), (a_last, 2),
     ]
     for work, i in order:
         work(i)
-    for i in range(nb):
-        out_copy(i).wait()
+    out_copy.wait()
 
     def drain_state(p, carry):
         @pl.when(z < nz - 1)
@@ -424,8 +455,10 @@
             ay_copy(d, a).wait_send()
         for d in range(1, nz):
             az_copy(d, a).wait_send()
-        for e in range(1, 2 * nx):
-            ag_copy(e, a).wait_send()
+        for d in range(1, nx):
+            ag_copy(d, a).wait_send()
+        for d in range(nx):
+            af_copy(d, a).wait_send()
     for b in range(len(SECOND)):
         for d in range(1, ny):
             by_copy(d, b).wait_send()
@@ -434,6 +467,24 @@
         for d in range(1, nx):
             bx_copy(d, b).wait_send()
         gb_copy(b).wait_send()
+
+
+PIECES = 8
+
+
+def hand_over(dx_ref, dw_ref, dx_out, dw_out, sem):
+    m = dx_ref.shape[0] // PIECES
+    copies = [
+        pltpu.make_async_copy(
+            dx_ref.at[pl.ds(i * m, m), :], dx_out.at[0, pl.ds(i * m, m), :], sem.at[i]
+        )
+        for i in range(PIECES)
+    ]
+    copies.append(pltpu.make_async_copy(dw_ref, dw_out, sem.at[PIECES]))
+    for copy in copies:
+        copy.start()
+    for copy in copies:
+        copy.wait()
 
 
 def shards(nz, ny, nx, inputs, weights, out_grad):
@@ -445,40 +496,48 @@
     V = pltpu.VMEM
     D = pltpu.SemaphoreType.DMA
     scratch = [
+        V((tok, dm), BF16), V(weights.shape, BF16), V(cot.shape, BF16), D((3 * H // 2 + 2,)), V((tok, 3 * HD), BF16),
         V((3, H, tok, HD), BF16), V((H, tok, HD), BF16),
         V((nb, H, HD, HD), F32), V((nb, H, HD, HD), F32),
         V((3, H, tok, HD), F32), V((tok, 3 * H * HD), BF16), V((dm, tok), BF16),
-        V((tok, dm), F32), D((nb,)),
+        V((tok, dm), BF16), D(()),
         V((2, H, HD, HD), F32), V((2, H, HD, HD), F32),
         V((ny - 1, H, HD, HD), F32), V((ny - 1, H, HD, HD), F32),
         V((4, 3, nz, ny, nx, rx, HD), F32), V((2, 3, nz, ny, nx, rx, HD), F32),
         V((nx - 1, na, nz, ny, rx, HD), F32), V((ny - 1, na, nz, rx, HD), F32),
-        V((na, nz, rx, HD), F32), V((nz - 1, na, rx, HD), F32), V((2 * nx, na, rx, HD), F32),
+        V((na, nz, rx, HD), F32), V((nz - 1, na, rx, HD), F32), V((2, nx, na, rx, HD), F32),
         V((ny - 1, ns, nz, nx, rx, HD), F32), V((nz - 1, ns, nx, rx, HD), F32),
         V((ns, nx, rx, HD), F32), V((nx - 1, ns, nx, rx, HD), F32),
         V((ns, nx, rx, HD), F32), V((ns, nx, rx, HD), F32),
         D((H,)), D((H,)), D((H,)), D((H,)),
         D((ny - 1, H)), D((ny - 1, H)), D((ny - 1, H)), D((ny - 1, H)),
         D((2, 3)), D((2, 3)), D((nx - 1, na)), D((nx - 1, na)), D((ny - 1, na)), D((ny - 1, na)),
-        D((nz - 1, na)), D((nz - 1, na)), D((2 * nx, na)), D((2 * nx, na)),
+        D((nz - 1, na)), D((nz - 1, na)), D((nx - 1, na)), D((nx - 1, na)), D((nx, na)), D((nx, na)),
         D((ny - 1, ns)), D((ny - 1, ns)), D((nz - 1, ns)), D((nz - 1, ns)),
         D((nx - 1, ns)), D((nx - 1, ns)), D((ns,)), D((ns,)),
     ]
     vm = pl.BlockSpec(memory_space=pltpu.VMEM)
+    hbm = pl.BlockSpec(memory_space=pl.ANY)
     dx, dw = pl.pallas_call(
         functools.partial(kernel, (nz, ny, nx)),
         out_shape=(
-            jax.ShapeDtypeStruct((tok, dm), F32),
+            jax.ShapeDtypeStruct((tok, dm), BF16),
             jax.ShapeDtypeStruct((dm // (nz * ny), weights.shape[1]), F32),
         ),
-        in_specs=[vm, vm, vm],
-        out_specs=(pl.BlockSpec(memory_space=pl.ANY), vm),
+        in_specs=[hbm, hbm, hbm],
+        out_specs=(hbm, vm),
         scratch_shapes=scratch,
         compiler_params=pltpu.CompilerParams(
             collective_id=0, has_side_effects=True, vmem_limit_bytes=60 * 1024 * 1024
         ),
     )(record, weights, cot)
-    return dx.astype(BF16)[None], dw
+    return pl.pallas_call(
+        hand_over,
+        out_shape=(jax.ShapeDtypeStruct((1, tok, dm), BF16), jax.ShapeDtypeStruct(dw.shape, F32)),
+        in_specs=[hbm, hbm],
+        out_specs=(hbm, hbm),
+        scratch_shapes=[D((PIECES + 1,))],
+    )(dx, dw)
 
 
 def solution(mesh):

time: 84.5 us -> 173 us (2.05)
  Pallas kernels: 78.9 us -> 173 us
  other arithmetic: 3.91 us -> 0 us
    pallas_call x0 -> x1, Pallas kernels: none -> 88.5 us  [shards(): pl.pallas_call(hand_over, out_shape=(jax.ShapeDtypeStruct((1, tok, dm), B...]
    pallas_call x1, Pallas kernels: 78.9 us -> 84 us  [shards(): pl.pallas_call(functools.partial(kernel, (nz, ny, nx)), out_shape=(jax.Sh...]
    broadcast_in_dim x1 -> x0, other arithmetic: 3.91 us -> none  [shards(): return (dx.astype(BF16)[None], dw)]
where the time goes in v3:
time: 173 us
  Pallas kernels  173 us (100%)
    pallas_call x1, Pallas kernels, shards(): pl.pallas_call(hand_over, out_shape=(jax.ShapeDtypeStruct((1, tok, dm), B...  88.5 us
    pallas_call x1, Pallas kernels, shards(): pl.pallas_call(functools.partial(kernel, (nz, ny, nx)), out_shape=(jax.Sh...  84 us

profile of v3, /device:TPU:0, one launch (start us, length us, event | category | flops | bytes accessed | tf_op | source)
XLA Modules:
  0.0 173.1 jit_solution(12915708768501147914)
XLA Ops:
  0.6 84.0 %shard_map.50 = (bf16[1024,1024]{1,0:T(8,128)(2,1)}, f32[128,1536]{1,0:T(8,128)}) custom-call(bf16[1024,1024]{1,0:T(8,128)(2,1)} %bitcast.2, bf16[1024,1536]{1,0:T(8,128)(2,1)} %w_hbm.1, bf16[1024,512]{1,0:T(8,128)(2,1)} %bitcast.3), custom_call_target="tpu_custom_call" | custom-call | tf_op jit(solution)/shard_map/pallas_call | solution.py:521
  84.6 88.5 %shard_map.51 = (bf16[1,1024,1024]{2,1,0:T(8,128)(2,1)}, f32[128,1536]{1,0:T(8,128)}) custom-call(bf16[1024,1024]{1,0:T(8,128)(2,1)} %get-tuple-element.4.dx_ref, f32[128,1536]{1,0:T(8,128)} %get-tuple-element.5.dw_ref), custom_call_target="tpu_custom_call" | custom-call | tf_op jit(solution)/shard_map/pallas_call | solution.py:534

commit v4 on v2

--- a/solution.py
+++ b/solution.py
@@ -22,18 +22,17 @@
     return lax.dot_general(a, b, dims, preferred_element_type=F32)
 
 
-FIRST = ((0, 0), (0, 1), (0, 2), (1, 0))
-SECOND = ((1, 1), (1, 2))
+GROUPS = tuple((slot, j) for slot in range(2) for j in range(3))
 
 
 def kernel(
     sizes,
     x_ref, w_ref, og_ref, dx_ref, dw_ref,
-    qkv, sc, kvg, qgg, loc, dqkv, xt, dxs, dx_sem,
+    dcat, qkv, sc, kvg, qgg, loc, dqkv, xt, dxs, dx_sem,
     kst, qst, kyr, qyr,
     part, crecv, a_xr, a_yr, a2, a_zr, ga, b_yr, b_zr, b2, b_xr, b3, gb,
     zk_s, zk_r, zq_s, zq_r, yk_s, yk_r, yq_s, yq_r,
-    c_s, c_r, ax_s, ax_r, ay_s, ay_r, az_s, az_r, ag_s, ag_r,
+    c_s, c_r, ax_s, ax_r, ay_s, ay_r, az_s, az_r, ag_s, ag_r, af_s, af_r,
     by_s, by_r, bz_s, bz_r, bx_s, bx_r, gb_s, gb_r,
 ):
     nz, ny, nx = sizes
@@ -73,7 +72,7 @@
 
     peers = [at(c_=1 - c)]
     for d in range(1, nx):
-        peers += [at(x_=xpeer(d)), at(x_=xpeer(d), c_=1 - c)]
+        peers += [at(x_=xpeer(d))]
     peers += [at(y_=ypeer(d)) for d in range(1, ny)]
     peers += [at(z_=zpeer(d)) for d in range(1, nz)]
     barrier = pltpu.get_barrier_semaphore()
@@ -157,13 +156,13 @@
     def ax_copy(d, a):
         o = xpeer(d)
         return remote(
-            mine(FIRST[a]).at[:, :, o], a_xr.at[d - 1, a], ax_s.at[d - 1, a], ax_r.at[d - 1, a], at(x_=o)
+            mine(GROUPS[a]).at[:, :, o], a_xr.at[d - 1, a], ax_s.at[d - 1, a], ax_r.at[d - 1, a], at(x_=o)
         )
 
     def ay_copy(d, a):
         o = ypeer(d)
         return remote(
-            mine(FIRST[a]).at[:, o, x], a_yr.at[d - 1, a], ay_s.at[d - 1, a], ay_r.at[d - 1, a], at(y_=o)
+            mine(GROUPS[a]).at[:, o, x], a_yr.at[d - 1, a], ay_s.at[d - 1, a], ay_r.at[d - 1, a], at(y_=o)
         )
 
     def az_copy(d, a):
@@ -173,13 +172,13 @@
     def by_copy(d, b):
         o = ypeer(d)
         return remote(
-            mine(SECOND[b]).at[:, o], b_yr.at[d - 1, b], by_s.at[d - 1, b], by_r.at[d - 1, b], at(y_=o)
+            mine(GROUPS[b]).at[:, o], b_yr.at[d - 1, b], by_s.at[d - 1, b], by_r.at[d - 1, b], at(y_=o)
         )
 
     def bz_copy(d, b):
         o = zpeer(d)
         return remote(
-            mine(SECOND[b]).at[o, y], b_zr.at[d - 1, b], bz_s.at[d - 1, b], bz_r.at[d - 1, b], at(z_=o)
+            mine(GROUPS[b]).at[o, y], b_zr.at[d - 1, b], bz_s.at[d - 1, b], bz_r.at[d - 1, b], at(z_=o)
         )
 
     def bx_copy(d, b):
@@ -189,11 +188,13 @@
     def gb_copy(b):
         return remote(b3.at[b], gb.at[b], gb_s.at[b], gb_r.at[b], at(c_=1 - c))
 
-    def ag_copy(e, j):
-        d, flip = e // 2, e % 2
-        o = xpeer(d)
-        oc = 1 - c if flip else c
-        return remote(ga.at[0, j], ga.at[e, j], ag_s.at[e, j], ag_r.at[e, j], at(x_=o, c_=oc))
+    def ag_copy(d, a):
+        return remote(
+            ga.at[0, 0, a], ga.at[0, d, a], ag_s.at[d - 1, a], ag_r.at[d - 1, a], at(x_=xpeer(d))
+        )
+
+    def af_copy(d, a):
+        return remote(ga.at[0, d, a], ga.at[1, d, a], af_s.at[d, a], af_r.at[d, a], at(c_=1 - c))
 
     def finish(p):
         hh = head(p)
@@ -208,6 +209,7 @@
             rows = pl.ds(n * CH, CH)
             dq = loc[0, p, rows, :] + mm(sc[hh, rows, :], start.astype(BF16), NT)
             dqkv[rows, cols[0]] = dq.astype(BF16)
+            dcat[rows, :HD] = dq.astype(BF16)
             start = start + kvg[n, hh]
         for n in range(nb - 1, -1, -1):
             rows = pl.ds(n * CH, CH)
@@ -216,18 +218,20 @@
             dv = loc[2, p, rows, :] + mm(qkv[1, hh, rows, :], after)
             dqkv[rows, cols[1]] = dk.astype(BF16)
             dqkv[rows, cols[2]] = dv.astype(BF16)
+            dcat[rows, HD : 2 * HD] = dk.astype(BF16)
+            dcat[rows, 2 * HD :] = dv.astype(BF16)
             end = end + qgg[n, hh]
-        d = jnp.concatenate([dqkv[:, cols[j]] for j in range(3)], axis=1)
-        zrows = dm // nz
+        zb = 2 if nz % 2 == 0 else 1
+        m = zb * (dm // nz)
 
         def slab(i, carry):
-            rows = pl.ds(pl.multiple_of(i * zrows, zrows), zrows)
-            r = mm(xt[rows, :], d)
+            rows = pl.ds(pl.multiple_of(i * m, m), m)
+            r = mm(xt[rows, :], dcat[...])
             for j in range(3):
-                part[p, j, i] = r[:, j * HD : (j + 1) * HD].reshape(ny, nx, rx, HD)
+                part[p, j, pl.ds(i * zb, zb)] = r[:, j * HD : (j + 1) * HD].reshape(zb, ny, nx, rx, HD)
             return carry
 
-        lax.fori_loop(0, nz, slab, 0)
+        lax.fori_loop(0, nz // zb, slab, 0)
 
     def head_step(p):
         finish(p)
@@ -246,14 +250,15 @@
                     part[p, j, i] = part[p, j, i] + crecv[slot, j, i]
                 for s_ in range(2):
 
-                    @pl.when(slot == s_)
+                    @pl.when((slot == s_) & (c == 0))
                     def _():
-                        if (s_, j) in FIRST:
-                            for d in range(1, nx):
-                                ax_copy(d, FIRST.index((s_, j))).start()
-                        else:
-                            for d in range(1, ny):
-                                by_copy(d, SECOND.index((s_, j))).start()
+                        for d in range(1, nx):
+                            ax_copy(d, GROUPS.index((s_, j))).start()
+
+                    @pl.when((slot == s_) & (c == 1))
+                    def _():
+                        for d in range(1, ny):
+                            by_copy(d, GROUPS.index((s_, j))).start()
 
     items = nb * (H + 1)
     per = 1
@@ -303,13 +308,13 @@
 
     def rows_of(i):
         rows = pl.ds(i * CH, CH)
-        dxs[rows, :] = mm(dqkv[rows, :], w_ref[...], NT)
+        dxs[rows, :] = mm(dqkv[rows, :], w_ref[...], NT).astype(BF16)
         out_copy(i).start()
 
     def a_one(a):
         for d in range(1, nx):
             ax_copy(d, a).wait_recv()
-        own = mine(FIRST[a])
+        own = mine(GROUPS[a])
         for i in range(nz):
             t = own[i, :, x]
             for d in range(1, nx):
@@ -321,7 +326,7 @@
     def a_two(a):
         for d in range(1, ny):
             ay_copy(d, a).wait_recv()
-        own = mine(FIRST[a])
+        own = mine(GROUPS[a])
         for i in range(nz):
             t = own[i, y, x]
             for d in range(1, ny):
@@ -336,26 +341,34 @@
         t = a2[a, z]
         for d in range(1, nz):
             t = t + a_zr[d - 1, a]
-        ga[0, a] = t
-        for e in range(1, 2 * nx):
-            ag_copy(e, a).start()
+        ga[0, 0, a] = t
+        for d in range(1, nx):
+            ag_copy(d, a).start()
+        af_copy(0, a).start()
 
     def cols_of(g, core):
         return pl.ds(pl.multiple_of(g[1] * width + (2 * core + g[0]) * HD, HD), HD)
 
+    def place(flip, d, a):
+        rows = pl.ds(pl.multiple_of(lax.rem(x - d + nx, nx) * rx, rx), rx)
+        dw_ref[rows, cols_of(GROUPS[a], 0)] = ga[flip, d, a]
+
+    def a_four(a):
+        for d in range(1, nx):
+            ag_copy(d, a).wait_recv()
+            af_copy(d, a).start()
+        for d in range(nx):
+            place(0, d, a)
+
     def a_last(a):
-        for e in range(2 * nx):
-            if e:
-                ag_copy(e, a).wait_recv()
-            d, flip = e // 2, e % 2
-            o = lax.rem(x - d + nx, nx)
-            rows = pl.ds(pl.multiple_of(o * rx, rx), rx)
-            dw_ref[rows, cols_of(FIRST[a], 1 - c if flip else c)] = ga[e, a]
+        for d in range(nx):
+            af_copy(d, a).wait_recv()
+            place(1, d, a)
 
     def b_one(b):
         for d in range(1, ny):
             by_copy(d, b).wait_recv()
-        own = mine(SECOND[b])
+        own = mine(GROUPS[b])
         for i in range(nz):
             t = own[i, y]
             for d in range(1, ny):
@@ -367,7 +380,7 @@
     def b_two(b):
         for d in range(1, nz):
             bz_copy(d, b).wait_recv()
-        t = mine(SECOND[b])[z, y]
+        t = mine(GROUPS[b])[z, y]
         for d in range(1, nz):
             t = t + b_zr[d - 1, b]
         b2[b] = t
@@ -382,20 +395,37 @@
             t = t + b_xr[d - 1, b]
         b3[b] = t
         gb_copy(b).start()
-        dw_ref[:, cols_of(SECOND[b], c)] = t.reshape(nx * rx, HD)
+        dw_ref[:, cols_of(GROUPS[b], 1)] = t.reshape(nx * rx, HD)
 
     def b_last(b):
         gb_copy(b).wait_recv()
-        dw_ref[:, cols_of(SECOND[b], 1 - c)] = gb[b].reshape(nx * rx, HD)
-
-    order = [
-        (a_one, 0), (rows_of, 0), (b_one, 0), (rows_of, 1), (a_one, 1), (rows_of, 2), (a_two, 0),
-        (rows_of, 3), (b_one, 1), (b_two, 0), (a_one, 2), (a_two, 1), (a_three, 0), (b_three, 0),
-        (a_one, 3), (a_two, 2), (b_two, 1), (a_three, 1), (b_three, 1), (a_two, 3), (a_three, 2),
-        (a_three, 3), (b_last, 0), (b_last, 1), (a_last, 0), (a_last, 1), (a_last, 2), (a_last, 3),
-    ]
-    for work, i in order:
-        work(i)
+        dw_ref[:, cols_of(GROUPS[b], 1)] = gb[b].reshape(nx * rx, HD)
+
+    count = len(GROUPS)
+
+    def waves(stages, gap):
+        order = []
+        for w in range(count + gap * len(stages)):
+            if w < nb:
+                order.append((rows_of, w))
+            for lag, stage in enumerate(stages):
+                if 0 <= w - gap * lag < count:
+                    order.append((stage, w - gap * lag))
+        for work, i in order:
+            work(i)
+
+    @pl.when(c == 0)
+    def _():
+        waves((a_one, a_two, a_three, a_four), 1)
+        for b in range(count):
+            b_last(b)
+
+    @pl.when(c == 1)
+    def _():
+        waves((b_one, b_two, b_three), 1)
+        for a in range(count):
+            a_last(a)
+
     for i in range(nb):
         out_copy(i).wait()
 
@@ -417,23 +447,30 @@
     for j in range(3):
         core_copy(0, j).wait_send()
         core_copy(1, j).wait_send()
-    for a in range(len(FIRST)):
-        for d in range(1, nx):
-            ax_copy(d, a).wait_send()
-        for d in range(1, ny):
-            ay_copy(d, a).wait_send()
-        for d in range(1, nz):
-            az_copy(d, a).wait_send()
-        for e in range(1, 2 * nx):
-            ag_copy(e, a).wait_send()
-    for b in range(len(SECOND)):
-        for d in range(1, ny):
-            by_copy(d, b).wait_send()
-        for d in range(1, nz):
-            bz_copy(d, b).wait_send()
-        for d in range(1, nx):
-            bx_copy(d, b).wait_send()
-        gb_copy(b).wait_send()
+
+    @pl.when(c == 0)
+    def _():
+        for a in range(count):
+            for d in range(1, nx):
+                ax_copy(d, a).wait_send()
+                ag_copy(d, a).wait_send()
+            for d in range(1, ny):
+                ay_copy(d, a).wait_send()
+            for d in range(1, nz):
+                az_copy(d, a).wait_send()
+            for d in range(nx):
+                af_copy(d, a).wait_send()
+
+    @pl.when(c == 1)
+    def _():
+        for b in range(count):
+            for d in range(1, ny):
+                by_copy(d, b).wait_send()
+            for d in range(1, nz):
+                bz_copy(d, b).wait_send()
+            for d in range(1, nx):
+                bx_copy(d, b).wait_send()
+            gb_copy(b).wait_send()
 
 
 def shards(nz, ny, nx, inputs, weights, out_grad):
@@ -441,44 +478,46 @@
     tok, dm = record.shape
     nb = tok // CH
     rx = dm // (nz * ny * nx)
-    na, ns = len(FIRST), len(SECOND)
+    na = ns = len(GROUPS)
     V = pltpu.VMEM
     D = pltpu.SemaphoreType.DMA
     scratch = [
+        V((tok, 3 * HD), BF16),
         V((3, H, tok, HD), BF16), V((H, tok, HD), BF16),
         V((nb, H, HD, HD), F32), V((nb, H, HD, HD), F32),
         V((3, H, tok, HD), F32), V((tok, 3 * H * HD), BF16), V((dm, tok), BF16),
-        V((tok, dm), F32), D((nb,)),
+        V((tok, dm), BF16), D((nb,)),
         V((2, H, HD, HD), F32), V((2, H, HD, HD), F32),
         V((ny - 1, H, HD, HD), F32), V((ny - 1, H, HD, HD), F32),
         V((4, 3, nz, ny, nx, rx, HD), F32), V((2, 3, nz, ny, nx, rx, HD), F32),
         V((nx - 1, na, nz, ny, rx, HD), F32), V((ny - 1, na, nz, rx, HD), F32),
-        V((na, nz, rx, HD), F32), V((nz - 1, na, rx, HD), F32), V((2 * nx, na, rx, HD), F32),
+        V((na, nz, rx, HD), F32), V((nz - 1, na, rx, HD), F32), V((2, nx, na, rx, HD), F32),
         V((ny - 1, ns, nz, nx, rx, HD), F32), V((nz - 1, ns, nx, rx, HD), F32),
         V((ns, nx, rx, HD), F32), V((nx - 1, ns, nx, rx, HD), F32),
         V((ns, nx, rx, HD), F32), V((ns, nx, rx, HD), F32),
         D((H,)), D((H,)), D((H,)), D((H,)),
         D((ny - 1, H)), D((ny - 1, H)), D((ny - 1, H)), D((ny - 1, H)),
         D((2, 3)), D((2, 3)), D((nx - 1, na)), D((nx - 1, na)), D((ny - 1, na)), D((ny - 1, na)),
-        D((nz - 1, na)), D((nz - 1, na)), D((2 * nx, na)), D((2 * nx, na)),
+        D((nz - 1, na)), D((nz - 1, na)), D((nx - 1, na)), D((nx - 1, na)), D((nx, na)), D((nx, na)),
         D((ny - 1, ns)), D((ny - 1, ns)), D((nz - 1, ns)), D((nz - 1, ns)),
         D((nx - 1, ns)), D((nx - 1, ns)), D((ns,)), D((ns,)),
     ]
     vm = pl.BlockSpec(memory_space=pltpu.VMEM)
+    hbm = pl.BlockSpec(memory_space=pl.ANY)
     dx, dw = pl.pallas_call(
         functools.partial(kernel, (nz, ny, nx)),
         out_shape=(
-            jax.ShapeDtypeStruct((tok, dm), F32),
+            jax.ShapeDtypeStruct((tok, dm), BF16),
             jax.ShapeDtypeStruct((dm // (nz * ny), weights.shape[1]), F32),
         ),
         in_specs=[vm, vm, vm],
-        out_specs=(pl.BlockSpec(memory_space=pl.ANY), vm),
+        out_specs=(hbm, vm),
         scratch_shapes=scratch,
         compiler_params=pltpu.CompilerParams(
             collective_id=0, has_side_effects=True, vmem_limit_bytes=60 * 1024 * 1024
         ),
     )(record, weights, cot)
-    return dx.astype(BF16)[None], dw
+    return dx[None], dw
 
 
 def solution(mesh):

time: 84.5 us -> 79.7 us (0.943); the launches traced: 84.4 us -> 78.5 us
  Pallas kernels: 78.9 us -> 73.8 us
  other arithmetic: 3.91 us -> 0 us
  local copies, waits for them, and re-layouts: 0.88 us -> 4.04 us
    pallas_call x1, Pallas kernels: 78.9 us -> 73.8 us  [shards(): pl.pallas_call(functools.partial(kernel, (nz, ny, nx)), out_shape=(jax.Sh...]
    broadcast_in_dim x1 -> x0, other arithmetic: 3.91 us -> none  [shards(): return (dx.astype(BF16)[None], dw)]
    unnamed x3 -> x4, local copies, waits for them, and re-layouts: 0.88 us -> 4.04 us
where the time goes in v4:
time: 79.7 us; the launch traced here: 78.5 us
  Pallas kernels  73.8 us (93%)
  local copies, waits for them, and re-layouts  4.04 us (5%)
    pallas_call x1, Pallas kernels, shards(): pl.pallas_call(functools.partial(kernel, (nz, ny, nx)), out_shape=(jax.Sh...  73.8 us
    unnamed x4, local copies, waits for them, and re-layouts  4.04 us

profile of v4, /device:TPU:0, one launch (start us, length us, event | category | flops | bytes accessed | tf_op | source)
XLA Modules:
  0.0 78.5 jit_solution(2562427872875741929)
XLA Ops:
  0.6 73.8 %shard_map.50 = (bf16[1024,1024]{1,0:T(8,128)(2,1)}, f32[128,1536]{1,0:T(8,128)}) custom-call(bf16[1024,1024]{1,0:T(8,128)(2,1)} %bitcast.3, bf16[1024,1536]{1,0:T(8,128)(2,1)} %w_ref.1, bf16[1024,512]{1,0:T(8,128)(2,1)} %bitcast.5), custom_call_target="tpu_custom_call" | custom-call | tf_op jit(solution)/shard_map/pallas_call | solution.py:507
  74.4 0.0 copy-start
  74.5 3.2 %copy.7 = bf16[1,1024,1024]{2,1,0:T(8,128)(2,1)} copy(bf16[1,1024,1024]{2,1,0:T(8,128)(2,1)} %bitcast.4) | data formatting | bytes 4194304
  77.6 0.0 copy-done
  77.6 0.9 %copy.8 = f32[128,1536]{1,0:T(8,128)} copy(f32[128,1536]{1,0:T(8,128)S(1)} %copy-done) | data formatting | bytes 1572864
Async XLA Ops:
  74.4 3.2 %copy-start = (f32[128,1536]{1,0:T(8,128)S(1)}, f32[128,1536]{1,0:T(8,128)}, u32[]{:S(2)}) copy-start(f32[128,1536]{1,0:T(8,128)} %get-tuple-element.9) | copy-start | bytes 2359300

commit v5 on v4

--- a/solution.py
+++ b/solution.py
@@ -471,6 +471,14 @@
             for d in range(1, nx):
                 bx_copy(d, b).wait_send()
             gb_copy(b).wait_send()
+
+
+BLOCKS = 4
+
+
+def hand_over(dx_ref, dw_ref, dx_out, dw_out):
+    dx_out[0] = dx_ref[...]
+    dw_out[...] = dw_ref[...]
 
 
 def shards(nz, ny, nx, inputs, weights, out_grad):
@@ -517,7 +525,14 @@
             collective_id=0, has_side_effects=True, vmem_limit_bytes=60 * 1024 * 1024
         ),
     )(record, weights, cot)
-    return dx[None], dw
+    m, k, wide = tok // BLOCKS, dw.shape[0] // BLOCKS, dw.shape[1]
+    return pl.pallas_call(
+        hand_over,
+        grid=(BLOCKS,),
+        out_shape=(jax.ShapeDtypeStruct((1, tok, dm), BF16), jax.ShapeDtypeStruct(dw.shape, F32)),
+        in_specs=[pl.BlockSpec((m, dm), lambda i: (i, 0)), pl.BlockSpec((k, wide), lambda i: (i, 0))],
+        out_specs=(pl.BlockSpec((1, m, dm), lambda i: (0, i, 0)), pl.BlockSpec((k, wide), lambda i: (i, 0))),
+    )(dx, dw)
 
 
 def solution(mesh):

time: 79.7 us -> 79.7 us (level)
  local copies, waits for them, and re-layouts: 4.04 us -> 0 us
  Pallas kernels: 73.8 us -> 77.8 us
    unnamed x4 -> x0, local copies, waits for them, and re-layouts: 4.04 us -> none
    pallas_call x0 -> x1, Pallas kernels: none -> 4.02 us  [shards(): pl.pallas_call(hand_over, grid=(BLOCKS,), out_shape=(jax.ShapeDtypeStruct...]
where the time goes in v5:
time: 79.7 us; the launch traced here: 78.5 us
  Pallas kernels  77.8 us (98%)
    pallas_call x1, Pallas kernels, shards(): pl.pallas_call(functools.partial(kernel, (nz, ny, nx)), out_shape=(jax.Sh...  73.8 us
    pallas_call x1, Pallas kernels, shards(): pl.pallas_call(hand_over, grid=(BLOCKS,), out_shape=(jax.ShapeDtypeStruct...  4.02 us

profile of v5, /device:TPU:0, one launch (start us, length us, event | category | flops | bytes accessed | tf_op | source)
XLA Modules:
  0.0 78.5 jit_solution(9239747244549674064)
XLA Ops:
  0.6 73.8 %shard_map.50 = (bf16[1024,1024]{1,0:T(8,128)(2,1)}, f32[128,1536]{1,0:T(8,128)}) custom-call(bf16[1024,1024]{1,0:T(8,128)(2,1)} %bitcast.2, bf16[1024,1536]{1,0:T(8,128)(2,1)} %w_ref.1, bf16[1024,512]{1,0:T(8,128)(2,1)} %bitcast.3), custom_call_target="tpu_custom_call" | custom-call | tf_op jit(solution)/shard_map/pallas_call | solution.py:515
  74.5 4.0 %shard_map.51 = (bf16[1,1024,1024]{2,1,0:T(8,128)(2,1)}, f32[128,1536]{1,0:T(8,128)}) custom-call(bf16[1024,1024]{1,0:T(8,128)(2,1)} %get-tuple-element.4.dx_ref, f32[128,1536]{1,0:T(8,128)} %get-tuple-element.5.dw_ref), custom_call_target="tpu_custom_call" | custom-call | tf_op jit(solution)/shard_map/pallas_call | solution.py:529

commit v6 on v4

--- a/solution.py
+++ b/solution.py
@@ -27,8 +27,8 @@
 
 def kernel(
     sizes,
-    x_ref, w_ref, og_ref, dx_ref, dw_ref,
-    dcat, qkv, sc, kvg, qgg, loc, dqkv, xt, dxs, dx_sem,
+    x_hbm, w_ref, og_hbm, dx_ref, dw_ref,
+    x_ref, og_ref, in_sem, dcat, qkv, sc, kvg, qgg, loc, dqkv, xt, dxs, dx_sem,
     kst, qst, kyr, qyr,
     part, crecv, a_xr, a_yr, a2, a_zr, ga, b_yr, b_zr, b2, b_xr, b3, gb,
     zk_s, zk_r, zq_s, zq_r, yk_s, yk_r, yq_s, yq_r,
@@ -79,8 +79,21 @@
     for peer in peers:
         pl.semaphore_signal(barrier, inc=1, device_id=peer, device_id_type=MESH)
 
+    def block_copies(n):
+        rows = pl.ds(pl.multiple_of(n * CH, CH), CH)
+        return (
+            pltpu.make_async_copy(x_hbm.at[rows, :], x_ref.at[rows, :], in_sem.at[0, n]),
+            pltpu.make_async_copy(og_hbm.at[rows, :], og_ref.at[rows, :], in_sem.at[1, n]),
+        )
+
+    for n in range(nb):
+        for copy in block_copies(n):
+            copy.start()
+
     def project(n, carry):
         rows = pl.ds(pl.multiple_of(n * CH, CH), CH)
+        for copy in block_copies(n):
+            copy.wait()
         r = mm(x_ref[rows, :], w_ref[...]).astype(BF16)
         pos = tm * tok + n * CH + lax.broadcasted_iota(jnp.int32, (CH, 1), 0)
         factor = 1.0 / jnp.sqrt(jnp.float32(HD) * (pos.astype(F32) + 1.0))
@@ -482,7 +495,7 @@
     V = pltpu.VMEM
     D = pltpu.SemaphoreType.DMA
     scratch = [
-        V((tok, 3 * HD), BF16),
+        V((tok, dm), BF16), V(cot.shape, BF16), D((2, nb)), V((tok, 3 * HD), BF16),
         V((3, H, tok, HD), BF16), V((H, tok, HD), BF16),
         V((nb, H, HD, HD), F32), V((nb, H, HD, HD), F32),
         V((3, H, tok, HD), F32), V((tok, 3 * H * HD), BF16), V((dm, tok), BF16),
@@ -510,7 +523,7 @@
             jax.ShapeDtypeStruct((tok, dm), BF16),
             jax.ShapeDtypeStruct((dm // (nz * ny), weights.shape[1]), F32),
         ),
-        in_specs=[vm, vm, vm],
+        in_specs=[hbm, vm, hbm],
         out_specs=(hbm, vm),
         scratch_shapes=scratch,
         compiler_params=pltpu.CompilerParams(

time: 79.7 us -> 80 us (level)
  no operation moved by 1% of the time
where the time goes in v6:
time: 80 us; the launch traced here: 78.7 us
  Pallas kernels  74 us (92%)
  local copies, waits for them, and re-layouts  4.04 us (5%)
    pallas_call x1, Pallas kernels, shards(): pl.pallas_call(functools.partial(kernel, (nz, ny, nx)), out_shape=(jax.Sh...  74 us
    unnamed x4, local copies, waits for them, and re-layouts  4.04 us

profile of v6, /device:TPU:0, one launch (start us, length us, event | category | flops | bytes accessed | tf_op | source)
XLA Modules:
  0.0 78.7 jit_solution(17972053373995733035)
XLA Ops:
  0.6 74.0 %shard_map.50 = (bf16[1024,1024]{1,0:T(8,128)(2,1)}, f32[128,1536]{1,0:T(8,128)}) custom-call(bf16[1024,1024]{1,0:T(8,128)(2,1)} %bitcast.3, bf16[1024,1536]{1,0:T(8,128)(2,1)} %w_ref.1, bf16[1024,512]{1,0:T(8,128)(2,1)} %bitcast.5), custom_call_target="tpu_custom_call" | custom-call | tf_op jit(solution)/shard_map/pallas_call | solution.py:520
  74.7 0.0 copy-start
  74.7 3.2 %copy.7 = bf16[1,1024,1024]{2,1,0:T(8,128)(2,1)} copy(bf16[1,1024,1024]{2,1,0:T(8,128)(2,1)} %bitcast.4) | data formatting | bytes 4194304
  77.8 0.0 copy-done
  77.9 0.9 %copy.8 = f32[128,1536]{1,0:T(8,128)} copy(f32[128,1536]{1,0:T(8,128)S(1)} %copy-done) | data formatting | bytes 1572864
Async XLA Ops:
  74.7 3.2 %copy-start = (f32[128,1536]{1,0:T(8,128)S(1)}, f32[128,1536]{1,0:T(8,128)}, u32[]{:S(2)}) copy-start(f32[128,1536]{1,0:T(8,128)} %get-tuple-element.9) | copy-start | bytes 2359300
